TPU v7x, 256 devices: a whole 4x4x8 slice. The times are simulated.
256 devices in a mesh: dp: 4 (over x), ctx: 64 (over z, y, core).
Axes of the slice: x: 4, y: 4, z: 8, core: 2. Of those that a mesh axis runs over, the one named last changes fastest.
Arguments:
- inputs: bfloat16 [4, 16384, 4096], P('dp', 'ctx'), may hold values from -6 to 6
- query_weight: bfloat16 [4096, 128], P('dp'), may hold values from -0.09375 to 0.09375
- key_weight: bfloat16 [4096, 128], P('dp'), may hold values from -0.09375 to 0.09375
- value_weight: bfloat16 [4096, 2048], P('dp'), may hold values from -0.09375 to 0.09375
- lambda_weight: bfloat16 [4096, 320], P('dp'), may hold values from -0.09375 to 0.09375
- log_decay: float32 [4, 16384, 16], P('dp', 'ctx'), may hold values from -1 to 0, as said below
- norm_gain: float32 [2048], replicated, may hold values from 0.5 to 1.5
Outputs:
- outputs: bfloat16 [4, 16384, 2048], P('dp', 'ctx')
Inputs may be any that keep to these rules, and one draw needn't show every extreme that they name: `log_decay`: entries are not positive.
All inputs are finite; a program needn't handle non-finite values.
Results may differ from a plain program's by a relative error of at most 0.0072.
Values may be sent and summed in bfloat16 or wider, within the bound.
No kernel may reach another device: no remote copies, remote signals or barrier semaphores. Data moves between devices by JAX's collectives and lax.ppermute only.
A program may use at most 128 MiB of HBM per device.

v0:
```python
import math

import jax
import jax.numpy as jnp
from jax import lax
from jax.sharding import PartitionSpec as P

HIGHEST = lax.Precision.HIGHEST


def from_partner(block, axis, stride):
    count = lax.axis_size(axis)
    route = []
    for low in range(count):
        high = low | 1 << stride
        if high != low and high < count:
            route += [(low, high), (high, low)]
    return lax.ppermute(block, axis, route)


def level_masks(length):
    depth = length.bit_length() - 1
    token_place = jnp.arange(length, dtype=jnp.int32)
    differ = jnp.bitwise_xor(token_place[:, None], token_place[None, :])
    level = jnp.zeros((length, length), jnp.int32)
    for power in range(depth):
        level = level + (differ >= 1 << power).astype(jnp.int32)
    levels = jnp.arange(depth + 1, dtype=jnp.int32)
    return (level[None, :, :] == levels[:, None, None]).astype(jnp.float32)


def block_terms(query_rows, key_rows, value_rows, lambdas, log_decay, masks):
    length, heads = log_decay.shape
    state_dim = query_rows.shape[1]
    head_dim = value_rows.shape[1] // heads
    inner = masks.shape[0]
    weights_all = lambdas.reshape(length, heads, -1)
    cumulative = jnp.cumsum(log_decay, axis=0)
    scores = lax.dot_general(
        query_rows, key_rows, (((1,), (1,)), ((), ())), preferred_element_type=jnp.float32
    ) / math.sqrt(state_dim)
    level_weight = jnp.einsum("lts,thl->hts", masks, weights_all[:, :, :inner], precision=HIGHEST)
    token_place = jnp.arange(length, dtype=jnp.int32)
    causal = token_place[:, None] >= token_place[None, :]
    spread = jnp.transpose(cumulative)
    distance = spread[:, :, None] - spread[:, None, :]
    decay = jnp.exp(jnp.where(causal[None], distance, -jnp.inf))
    mix = (level_weight * decay * scores[None]).astype(jnp.bfloat16)
    values = value_rows.reshape(length, heads, head_dim)
    near = jnp.einsum("hts,shd->thd", mix, values, preferred_element_type=jnp.float32)
    remain = jnp.exp(cumulative[-1][None, :] - cumulative)
    keyed = (key_rows.astype(jnp.float32)[:, None, :] * remain[:, :, None]).astype(jnp.bfloat16)
    state = jnp.einsum("chs,chd->hsd", keyed, values, preferred_element_type=jnp.float32)
    total = jnp.exp(cumulative[-1])
    return (near, state, total, cumulative, weights_all)


def finish(mixed, norm_gain):
    heads = mixed.shape[-2]
    mean_square = jnp.mean(mixed * mixed, axis=-1, keepdims=True)
    return (mixed * lax.rsqrt(mean_square + 1e-05) * norm_gain.reshape(heads, -1)).astype(
        jnp.bfloat16
    )


def make_fold(tokens):

    def accumulate(totals, pieces, start):
        return tuple(
            (jnp.dot(tokens, piece, preferred_element_type=jnp.float32) for piece in pieces)
        )

    return accumulate


def zeros_for(length, weights):
    return tuple((jnp.zeros((length, weight.shape[1]), jnp.float32) for weight in weights))


def per_device(inputs, query_weight, key_weight, value_weight, lambda_weight, log_decay, norm_gain):
    tokens = inputs[0]
    decays = log_decay[0]
    length = tokens.shape[0]
    accumulate = make_fold(tokens)
    query_sum, key_sum, value_sum, lambda_sum = accumulate(
        zeros_for(length, (query_weight, key_weight, value_weight, lambda_weight)),
        (
            lax.all_gather(query_weight, "dp", axis=0, tiled=True),
            lax.all_gather(key_weight, "dp", axis=0, tiled=True),
            lax.all_gather(value_weight, "dp", axis=0, tiled=True),
            lax.all_gather(lambda_weight, "dp", axis=0, tiled=True),
        ),
        jnp.int32(0),
    )
    query_rows = query_sum.astype(jnp.bfloat16)
    key_rows = key_sum.astype(jnp.bfloat16)
    value_rows = value_sum.astype(jnp.bfloat16)
    lambdas = jax.nn.softplus(lambda_sum)
    masks = level_masks(length)
    inner = masks.shape[0]
    scale = 1.0 / math.sqrt(query_rows.shape[1])
    near, state, total, cumulative, weights_all = block_terms(
        query_rows, key_rows, value_rows, lambdas, decays, masks
    )
    index = lax.axis_index("ctx")
    bits = lax.axis_size("ctx").bit_length() - 1
    block_state = state
    block_total = total
    carry_decay = jnp.ones_like(total)
    growth = jnp.exp(cumulative)
    mixed = near
    for level_bit in range(bits):
        other_state, other_total = from_partner((block_state, block_total), "ctx", level_bit)
        upper = (index >> level_bit & 1).astype(jnp.float32)
        carried = (carry_decay[:, None, None] * other_state).astype(jnp.bfloat16)
        reach = jnp.einsum("ts,hsd->thd", query_rows, carried, preferred_element_type=jnp.float32)
        factor = weights_all[:, :, inner + level_bit] * growth * (scale * upper)
        mixed = mixed + factor[..., None] * reach
        if level_bit + 1 < bits:
            block_state = jnp.where(
                upper > 0,
                block_total[:, None, None] * other_state + block_state,
                other_total[:, None, None] * block_state + other_state,
            )
            carry_decay = jnp.where(upper > 0, other_total * carry_decay, carry_decay)
            block_total = block_total * other_total
    return finish(mixed, norm_gain).reshape(1, length, -1)


def solution(mesh):
    return jax.shard_map(
        per_device,
        mesh=mesh,
        in_specs=(
            P("dp", "ctx", None),
            P("dp", None),
            P("dp", None),
            P("dp", None),
            P("dp", None),
            P("dp", "ctx", None),
            P(),
        ),
        out_specs=P("dp", "ctx", None),
        check_vma=False,
    )
```

profile of v0, /device:TPU:1, one launch (start us, length us, event | category | flops | bytes accessed | tf_op | source)
XLA Modules:
  0.0 458.8 jit_solution(10202419799631526548)
XLA Ops:
  9.9 28.7 %all-gather.11.cloned.1.call-done = bf16[4096,128]{1,0:T(8,128)(2,1)} async-done(((bf16[1024,128]{1,0:T(8,128)(2,1)}), bf16[4096,128]{1,0:T(8,128)(2,1)}) %all-gather.11.cloned.1.call-update) | async-done | bytes 1048592 | tf_op jit(solution)/shard_map/all_gather | solution.py:89
  40.6 38.7 %all-gather.7.cloned.1.call-done = bf16[4096,320]{0,1:T(8,128)(2,1)} async-done(((bf16[1024,320]{0,1:T(8,128)(2,1)}), bf16[4096,320]{0,1:T(8,128)(2,1)}) %all-gather.7.cloned.1.call-update) | async-done | bytes 2621456 | tf_op jit(solution)/shard_map/all_gather | solution.py:91
  79.4 2.7 compare_select_fusion
  83.0 155.1 %all-gather.5.cloned.1.call-done = bf16[4096,2048]{1,0:T(8,128)(2,1)} async-done(((bf16[1024,2048]{1,0:T(8,128)(2,1)}), bf16[4096,2048]{1,0:T(8,128)(2,1)}) %all-gather.5.cloned.1.call-update) | async-done | bytes 16777232 | tf_op jit(solution)/shard_map/all_gather | solution.py:90
  238.1 8.3 %fusion.18 = bf16[32,16,8,128]{3,2,1,0:T(8,128)(2,1)S(1)} fusion(bf16[4096,2048]{1,0:T(8,128)(2,1)} %all-gather.5.cloned.1.call-done, bf16[1,256,4096]{2,1,0:T(8,128)(2,1)S(1)} %copy-done), kind=kOutput, calls=%fused_computation.25 | convolution fusion | flops 4295491584 | bytes 19922944 | tf_op jit(solution)/shard_map/dot_general | solution.py:70
  250.9 3.0 fusion.57
  255.5 23.0 %collective-permute-done.3 = f32[16]{0:T(128)S(1)} collective-permute-done((f32[16]{0:T(128)S(1)}, f32[16]{0:T(128)S(1)}, u32[]{:S(2)}, u32[]{:S(2)}) %collective-permute-start.3) | collective-permute-done | bytes 96 | tf_op jit(solution)/shard_map/ppermute | solution.py:18
  278.4 2.7 collective-permute-start.5
  288.7 2.8 multiply_convert_fusion.7
  291.5 2.7 collective-permute-start.4
  294.2 19.0 %collective-permute-done.4 = f32[16,128,128]{2,1,0:T(8,128)S(1)} collective-permute-done((f32[16,128,128]{2,1,0:T(8,128)}, f32[16,128,128]{2,1,0:T(8,128)S(1)}, u32[]{:S(2)}, u32[]{:S(2)}) %collective-permute-start.4) | collective-permute-done | bytes 1048608 | tf_op jit(solution)/shard_map/ppermute | solution.py:18
  314.2 2.7 multiply_convert_fusion.6
  320.5 2.9 all-gather.9.cloned.1.call-done
  325.3 10.8 %collective-permute-done.6 = f32[16,128,128]{2,1,0:T(8,128)} collective-permute-done((f32[16,128,128]{2,1,0:T(8,128)S(1)}, f32[16,128,128]{2,1,0:T(8,128)}, u32[]{:S(2)}, u32[]{:S(2)}) %collective-permute-start.6) | collective-permute-done | bytes 1048608 | tf_op jit(solution)/shard_map/ppermute | solution.py:18
  336.2 2.7 multiply_convert_fusion.5
  343.4 4.5 fusion.1
  350.9 2.8 fusion.59
  355.7 30.0 %collective-permute-done.8 = f32[16,128,128]{2,1,0:T(8,128)} collective-permute-done((f32[16,128,128]{2,1,0:T(8,128)S(1)}, f32[16,128,128]{2,1,0:T(8,128)}, u32[]{:S(2)}, u32[]{:S(2)}) %collective-permute-start.8) | collective-permute-done | bytes 1048608 | tf_op jit(solution)/shard_map/ppermute | solution.py:18
  385.8 2.8 multiply_convert_fusion.4
  388.5 7.1 %collective-permute-start.10 = (f32[16,128,128]{2,1,0:T(8,128)}, f32[16,128,128]{2,1,0:T(8,128)}, u32[]{:S(2)}, u32[]{:S(2)}) collective-permute-start(f32[16,128,128]{2,1,0:T(8,128)} %get-tuple-element.21), channel_id=1, source_target_pairs={{0,32},{32,0},{1,33},{33,1},{2,34},{34,2},{3,35},{35,3},{4,36},{36... | collective-permute-start | bytes 3145736 | tf_op jit(solution)/shard_map/ppermute | solution.py:18
  398.4 2.8 fusion.61
  402.3 2.9 fusion.62
  407.2 34.3 %collective-permute-done.10 = f32[16,128,128]{2,1,0:T(8,128)} collective-permute-done((f32[16,128,128]{2,1,0:T(8,128)}, f32[16,128,128]{2,1,0:T(8,128)}, u32[]{:S(2)}, u32[]{:S(2)}) %collective-permute-start.10) | collective-permute-done | bytes 1048608 | tf_op jit(solution)/shard_map/ppermute | solution.py:18
  444.8 5.6 %multiply_reduce_fusion = (f32[256,16]{0,1:T(8,128)S(1)}, f32[256,16,128]{0,2,1:T(8,128)S(1)}) fusion(f32[256,16]{0,1:T(8,128)S(1)} %copy-done.17, f32[256,16]{0,1:T(8,128)S(1)} %copy-done.16, f32[256,16]{0,1:T(8,128)S(1)} %copy-done.15, f32[256,16]{0,1:T(8,128)S(1)} %copy-done.14, f32[256,16]{0,1:T(8,128)S(1)} %copy-done.13, ...), kind=kLoop, calls=%fused_computation.22 | loop fusion | flops 7335936 | bytes 16891904 | tf_op jit(solution)/shard_map/reduce_sum | solution.py:60
  (123 shorter events, 46.7 us)
Async XLA Ops:
  6.5 32.1 %copy-start = (bf16[1,256,4096]{2,1,0:T(8,128)(2,1)S(1)}, bf16[1,256,4096]{2,1,0:T(8,128)(2,1)}, u32[]{:S(2)}) copy-start(bf16[1,256,4096]{2,1,0:T(8,128)(2,1)} %param.7) | copy-start | bytes 6291460
  6.5 32.1 %all-gather.11.cloned.1.call-start = ((), (), s32[]{:S(2)}) async-start(), calls=%async_computation.3 | async-start | bytes 1310720 | tf_op jit(solution)/shard_map/all_gather | solution.py:89
  7.3 72.1 %all-gather.7.cloned.1.call-start = ((), (), s32[]{:S(2)}) async-start(), calls=%async_computation.1 | async-start | bytes 3276800 | tf_op jit(solution)/shard_map/all_gather | solution.py:91
  8.0 230.0 %all-gather.5.cloned.1.call-start = ((), (), s32[]{:S(2)}) async-start(), calls=%async_computation | async-start | bytes 20971520 | tf_op jit(solution)/shard_map/all_gather | solution.py:90
  8.8 314.6 %all-gather.9.cloned.1.call-start = ((), (), s32[]{:S(2)}) async-start(), calls=%async_computation.2 | async-start | bytes 1310720 | tf_op jit(solution)/shard_map/all_gather | solution.py:88
  9.7 308.5 %copy-start.18 = (f32[16,256]{1,0:T(8,128)}, f32[16,256]{1,0:T(8,128)S(1)}, u32[]{:S(2)}) copy-start(f32[16,256]{1,0:T(8,128)S(1)} %get-tuple-element.28) | copy-start | bytes 49156
  82.1 164.2 %copy-start.8 = (f32[256,16,20]{0,2,1:T(8,128)}, f32[256,16,20]{0,2,1:T(8,128)S(1)}, u32[]{:S(2)}) copy-start(f32[256,16,20]{0,2,1:T(8,128)S(1)} %reshape.125) | copy-start | bytes 983044
  247.8 3.2 collective-permute-start
  248.5 2.1 collective-permute-start.1
  254.0 34.8 %collective-permute-start.2 = (f32[16,128,128]{2,1,0:T(8,128)S(1)}, f32[16,128,128]{2,1,0:T(8,128)}, u32[]{:S(2)}, u32[]{:S(2)}) collective-permute-start(f32[16,128,128]{2,1,0:T(8,128)S(1)} %get-tuple-element.13), channel_id=1, source_target_pairs={{0,2},{2,0},{1,3},{3,1},{4,6},{6,4},{5,7},{7,5},{8,10},{10,8},{9,1... | collective-permute-start | bytes 3145736 | tf_op jit(solution)/shard_map/ppermute | solution.py:18
  255.2 23.3 %collective-permute-start.3 = (f32[16]{0:T(128)S(1)}, f32[16]{0:T(128)S(1)}, u32[]{:S(2)}, u32[]{:S(2)}) collective-permute-start(f32[16]{0:T(128)S(1)} %exponential_multiply_fusion), channel_id=1, source_target_pairs={{0,2},{2,0},{1,3},{3,1},{4,6},{6,4},{5,7},{7,5},{8,10},{10,8},{9,1... | collective-permute-start | bytes 200 | tf_op jit(solution)/shard_map/ppermute | solution.py:18
  278.4 3.9 collective-permute-start.5
  282.4 2.4 collective-permute-start.7
  284.7 32.1 %copy-start.25 = (f32[16]{0:T(128)}, f32[16]{0:T(128)S(1)}, u32[]{:S(2)}) copy-start(f32[16]{0:T(128)S(1)} %collective-permute-done.7) | copy-start | bytes 196
  284.8 3.4 collective-permute-start.9
  291.5 21.7 %collective-permute-start.4 = (f32[16,128,128]{2,1,0:T(8,128)}, f32[16,128,128]{2,1,0:T(8,128)S(1)}, u32[]{:S(2)}, u32[]{:S(2)}) collective-permute-start(f32[16,128,128]{2,1,0:T(8,128)} %get-tuple-element.15), channel_id=1, source_target_pairs={{0,4},{4,0},{1,5},{5,1},{2,6},{6,2},{3,7},{7,3},{8,12},{12,8},{9,1... | collective-permute-start | bytes 3145736 | tf_op jit(solution)/shard_map/ppermute | solution.py:18
  316.9 19.3 %collective-permute-start.6 = (f32[16,128,128]{2,1,0:T(8,128)S(1)}, f32[16,128,128]{2,1,0:T(8,128)}, u32[]{:S(2)}, u32[]{:S(2)}) collective-permute-start(f32[16,128,128]{2,1,0:T(8,128)S(1)} %get-tuple-element.17), channel_id=1, source_target_pairs={{0,8},{8,0},{1,9},{9,1},{2,10},{10,2},{3,11},{11,3},{4,12},{12,4},... | collective-permute-start | bytes 3145736 | tf_op jit(solution)/shard_map/ppermute | solution.py:18
  338.9 46.9 %collective-permute-start.8 = (f32[16,128,128]{2,1,0:T(8,128)S(1)}, f32[16,128,128]{2,1,0:T(8,128)}, u32[]{:S(2)}, u32[]{:S(2)}) collective-permute-start(f32[16,128,128]{2,1,0:T(8,128)S(1)} %get-tuple-element.19), channel_id=1, source_target_pairs={{0,16},{16,0},{1,17},{17,1},{2,18},{18,2},{3,19},{19,3},{4,20},{20... | collective-permute-start | bytes 3145736 | tf_op jit(solution)/shard_map/ppermute | solution.py:18
  350.8 34.9 %copy-start.23 = (f32[16]{0:T(128)S(1)}, f32[16]{0:T(128)}, u32[]{:S(2)}) copy-start(f32[16]{0:T(128)} %copy-done.22) | copy-start | bytes 196
  350.8 34.9 %copy-start.24 = (f32[16]{0:T(128)S(1)}, f32[16]{0:T(128)}, u32[]{:S(2)}) copy-start(f32[16]{0:T(128)} %get-tuple-element.8) | copy-start | bytes 196
  350.9 34.9 %copy-start.28 = (f32[16]{0:T(128)S(1)}, f32[16]{0:T(128)}, u32[]{:S(2)}) copy-start(f32[16]{0:T(128)} %copy-done.27) | copy-start | bytes 196
  355.7 39.9 %copy-start.7 = (bf16[16,128,128]{1,2,0:T(8,128)(2,1)S(1)}, bf16[16,128,128]{1,2,0:T(8,128)(2,1)}, u32[]{:S(2)}) copy-start(bf16[16,128,128]{1,2,0:T(8,128)(2,1)} %copy.62) | copy-start | bytes 1572868
  388.5 53.0 %collective-permute-start.10 = (f32[16,128,128]{2,1,0:T(8,128)}, f32[16,128,128]{2,1,0:T(8,128)}, u32[]{:S(2)}, u32[]{:S(2)}) collective-permute-start(f32[16,128,128]{2,1,0:T(8,128)} %get-tuple-element.21), channel_id=1, source_target_pairs={{0,32},{32,0},{1,33},{33,1},{2,34},{34,2},{3,35},{35,3},{4,36},{36... | collective-permute-start | bytes 3145736 | tf_op jit(solution)/shard_map/ppermute | solution.py:18
  405.1 36.4 %copy-start.21 = (f32[16]{0:T(128)S(1)}, f32[16]{0:T(128)}, u32[]{:S(2)}) copy-start(f32[16]{0:T(128)} %get-tuple-element.7) | copy-start | bytes 196
  (22 other events, 111.1 us)
Sparse Core Ops, SparseCore 0:
  9.2 29.3 all-gather.10
  40.4 38.9 all-gather.6
  81.2 156.8 all-gather.4
  294.4 28.9 all-gather.8
where the time goes:
time: 459 us
  waiting for transfers between devices  350 us (76%)
  matrix products  34 us (7%)
  other arithmetic  24.9 us (5%)
  starting transfers between devices  22.3 us (5%)
  local copies, waits for them, and re-layouts  13.9 us (3%)
  between operations  13.5 us (3%)
    all_gather x1, waiting for transfers between devices, per_device(): lax.all_gather(value_weight, 'dp', axis=0, tiled=True)  155 us
    ppermute x11, waiting for transfers between devices, from_partner(): return lax.ppermute(block, axis, route)  123 us
    all_gather x1, waiting for transfers between devices, per_device(): lax.all_gather(lambda_weight, 'dp', axis=0, tiled=True)  38.7 us
    all_gather x1, waiting for transfers between devices, per_device(): lax.all_gather(key_weight, 'dp', axis=0, tiled=True)  28.7 us
    ppermute x11, starting transfers between devices, from_partner(): return lax.ppermute(block, axis, route)  22.1 us
    convert_element_type x6, other arithmetic, per_device(): carried = (carry_decay[:, None, None] * other_state).astype(jnp.bfloat16)  15.4 us
    dot_general x4, matrix products, accumulate(): jnp.dot(tokens, piece, preferred_element_type=jnp.float32)  14.8 us
    unnamed x6, matrix products  12.5 us
  transfers between devices with their start and end apart: 15, of which 14 were waited for; matrix products, arithmetic and copies ran while one was open for 9% of the time, Pallas kernels for 0%

commit v1 on v0

v1 whole, which is shorter than its diff:
```python
import functools
import math

import jax
import jax.numpy as jnp
from jax import lax
from jax.experimental import pallas as pl
from jax.experimental.pallas import tpu as pltpu
from jax.sharding import PartitionSpec as P

HIGHEST = lax.Precision.HIGHEST
F32 = jnp.float32
BF16 = jnp.bfloat16
BLOCK = 256
HALF = 128
LEVELS = 20
INNER = 9
BITS = 6
MASKS = (2, 6, 8, 24, 56)
HPC = 8
HPT = 6
VMEM_LIMIT = 56 * 1024 * 1024


def ring_x(step, n_dp, n_ctx):
    pairs = []
    for x in range(n_dp):
        for c in range(n_ctx):
            to = (x + (step if c % 2 == 0 else -step)) % n_dp
            pairs.append((x * n_ctx + c, to * n_ctx + c))
    return pairs


def ring_y(step, n_ctx):
    pairs = []
    for c in range(n_ctx):
        z, y, core = c >> 3, c >> 1 & 3, c & 1
        to = (y + (step if core == 0 else -step)) % 4
        pairs.append((c, z * 8 + to * 2 + core))
    return pairs


def xor_pairs(mask, n_ctx):
    return [(c, c ^ mask) for c in range(n_ctx)]


def whole(n):
    return [pl.BlockSpec(memory_space=pltpu.VMEM)] * n


def call(kernel, outs, args, smem=0, flops=0, nbytes=0, scratch=()):
    specs = [pl.BlockSpec(memory_space=pltpu.SMEM)] * smem + whole(len(args) - smem)
    return pl.pallas_call(
        kernel,
        out_shape=outs,
        in_specs=specs,
        out_specs=jax.tree.map(lambda _: pl.BlockSpec(memory_space=pltpu.VMEM), outs),
        scratch_shapes=list(scratch),
        compiler_params=pltpu.CompilerParams(vmem_limit_bytes=VMEM_LIMIT),
        cost_estimate=pl.CostEstimate(flops=flops, bytes_accessed=nbytes, transcendentals=0),
    )(*args)


def lam_slot(h):
    return h // HPT * HALF + h % HPT * LEVELS


def small_kernel(n, off_ref, tok_ref, gl_ref, *refs):
    pieces, (q_ref, k_ref, lam_ref) = refs[:n], refs[n:]
    total = None
    for p in range(n):
        depth = pieces[p].shape[0]
        columns = pl.ds(pl.multiple_of(off_ref[p], 256), depth)
        part = jnp.dot(tok_ref[:, columns], pieces[p][...], preferred_element_type=F32)
        total = part if total is None else total + part
    q_ref[...] = total[:, :HALF].astype(BF16)
    k_ref[...] = total[:, HALF : 2 * HALF].astype(BF16)
    lam = total[:, 2 * HALF :]
    soft = jnp.maximum(lam, 0.0) + jnp.log1p(jnp.exp(-jnp.abs(lam)))
    lam_ref[...] = soft * gl_ref[...]


def value_kernel(n, first, off_ref, tok_ref, *refs):
    base = None
    if not first:
        base, refs = refs[0], refs[1:]
    pieces, out_ref = refs[:n], refs[n]
    width = out_ref.shape[1]

    @pl.loop(0, width // 256)
    def _(j):
        cols = pl.ds(pl.multiple_of(j * 256, 256), 256)
        total = None if first else base[:, cols]
        for p in range(n):
            depth = pieces[p].shape[0]
            rows = pl.ds(pl.multiple_of(off_ref[p], 256), depth)
            part = jnp.dot(tok_ref[:, rows], pieces[p][:, cols], preferred_element_type=F32)
            total = part if total is None else total + part
        out_ref[:, cols] = total.astype(out_ref.dtype)


def state_kernel(k_ref, v_ref, remain_ref, tot_ref, chip_ref, low_ref):
    kt = jnp.transpose(k_ref[...].astype(F32))
    for h in range(HPC):
        cols = slice(h * HALF, (h + 1) * HALF)
        keyed = (kt * remain_ref[h : h + 1, :]).astype(BF16)
        low = jnp.dot(keyed[:, :BLOCK], v_ref[:BLOCK, cols], preferred_element_type=F32)
        high = jnp.dot(keyed[:, BLOCK:], v_ref[BLOCK:, cols], preferred_element_type=F32)
        low_ref[:, cols] = low.astype(BF16)
        chip_ref[:, cols] = tot_ref[h : h + 1, :] * low + high


def near_kernel(q_ref, k_ref, v_ref, lam_ref, cum_ref, cumt_ref, low_ref, out_ref):
    row = lax.broadcasted_iota(jnp.int32, (HALF, HALF), 0)
    col = lax.broadcasted_iota(jnp.int32, (HALF, HALF), 1)
    differ = jnp.bitwise_xor(row, col)
    level = jnp.zeros((HALF, HALF), jnp.int32)
    for power in range(7):
        level = level + jnp.where(differ >= 1 << power, 1, 0)
    causal = row >= col
    for b in range(2):
        r0 = b * BLOCK
        tiles = [slice(r0, r0 + HALF), slice(r0 + HALF, r0 + BLOCK)]
        scores = lax.dot_general(
            q_ref[r0 : r0 + BLOCK, :],
            k_ref[r0 : r0 + BLOCK, :],
            (((1,), (1,)), ((), ())),
            preferred_element_type=F32,
        )
        s00, s10, s11 = scores[:HALF, :HALF], scores[HALF:, :HALF], scores[HALF:, HALF:]
        for h in range(HPC):
            cols = slice(h * HALF, (h + 1) * HALF)
            slot = lam_slot(h)
            tile = slice(slot // HALF * HALF, slot // HALF * HALF + HALF)
            inner = slot % HALF
            lam0 = lam_ref[tiles[0], tile]
            lam1 = lam_ref[tiles[1], tile]
            index = level + inner
            w00 = jnp.take_along_axis(lam0, index, axis=1)
            w11 = jnp.take_along_axis(lam1, index, axis=1)
            w10 = jnp.broadcast_to(lam1[:, inner + 8 : inner + 9], (HALF, HALF))
            t0 = cum_ref[tiles[0], h : h + 1]
            t1 = cum_ref[tiles[1], h : h + 1]
            c0 = cumt_ref[h : h + 1, tiles[0]]
            c1 = cumt_ref[h : h + 1, tiles[1]]
            m00 = w00 * jnp.exp(jnp.where(causal, t0 - c0, -jnp.inf)) * s00
            m11 = w11 * jnp.exp(jnp.where(causal, t1 - c1, -jnp.inf)) * s11
            m10 = w10 * jnp.exp(t1 - c0) * s10
            v0 = v_ref[tiles[0], cols]
            v1 = v_ref[tiles[1], cols]
            out0 = jnp.dot(m00.astype(BF16), v0, preferred_element_type=F32)
            mix1 = jnp.concatenate([m10.astype(BF16), m11.astype(BF16)], axis=1)
            out1 = jnp.dot(mix1, v_ref[r0 : r0 + BLOCK, cols], preferred_element_type=F32)
            if b == 1:
                reach = jnp.dot(
                    q_ref[BLOCK:, :], low_ref[:, cols], preferred_element_type=F32
                )
                out0 = out0 + lam0[:, inner + INNER : inner + INNER + 1] * reach[:HALF]
                out1 = out1 + lam1[:, inner + INNER : inner + INNER + 1] * reach[HALF:]
            out_ref[tiles[0], cols] = out0
            out_ref[tiles[1], cols] = out1


def far_kernel(bits, last, q_ref, lam_ref, gain_ref, base_ref, *refs):
    carried, out_ref = refs[:-1], refs[-1]
    for h in range(HPC):
        cols = slice(h * HALF, (h + 1) * HALF)
        total = base_ref[:, cols]
        slot = lam_slot(h) + INNER
        for bit, ref in zip(bits, carried):
            reach = jnp.dot(q_ref[...], ref[:, cols], preferred_element_type=F32)
            total = total + lam_ref[:, slot + bit : slot + bit + 1] * reach
        if last:
            mean = jnp.mean(total * total, axis=1, keepdims=True)
            total = total * lax.rsqrt(mean + 1e-05) * gain_ref[:, cols]
        out_ref[:, cols] = total.astype(out_ref.dtype)


def per_device(inputs, query_weight, key_weight, value_weight, lambda_weight, log_decay, norm_gain):
    n_dp, n_ctx = lax.axis_size("dp"), lax.axis_size("ctx")
    x, ctx = lax.axis_index("dp"), lax.axis_index("ctx")
    core, y = ctx & 1, ctx >> 1 & 3
    sign = 1 - 2 * core
    rows = query_weight.shape[0]
    chunk = rows // 4
    half = value_weight.shape[1] // 2

    def px(a, step):
        return lax.ppermute(a, ("dp", "ctx"), ring_x(step, n_dp, n_ctx))

    def py(a, step):
        return lax.ppermute(a, "ctx", ring_y(step, n_ctx))

    def swap(a, mask):
        return lax.ppermute(a, "ctx", xor_pairs(mask, n_ctx))

    def in_order(mine, other, axis=0):
        low = jnp.where(core == 0, mine, other)
        high = jnp.where(core == 0, other, mine)
        return jnp.concatenate([low, high], axis=axis)

    mine = lax.dynamic_slice(value_weight, (y * chunk, core * half), (chunk, half))
    a1 = px(mine, 1)
    a2 = px(mine, -1)
    a3 = px(a1, 1)
    lam_half = lax.dynamic_slice(lambda_weight, (0, core * HPC * LEVELS), (rows, HPC * LEVELS))
    cut = HPT * LEVELS
    small = jnp.concatenate(
        [
            query_weight,
            key_weight,
            jnp.pad(lam_half[:, :cut], ((0, 0), (0, HALF - cut))),
            jnp.pad(lam_half[:, cut:], ((0, 0), (0, HALF - (HPC * LEVELS - cut)))),
        ],
        axis=1,
    )
    s1 = px(small, 1)
    s2 = px(small, -1)
    s3 = px(s1, 1)
    tokens = in_order(inputs[0], swap(inputs[0], 1))
    decay_mine = log_decay[0]
    decays = in_order(decay_mine, swap(decay_mine, 1))
    decays = lax.dynamic_slice(decays, (0, core * HPC), (2 * BLOCK, HPC))

    sources = [(a1, (x - sign) % n_dp), (a2, (x + sign) % n_dp), (a3, x ^ 2)]
    pieces, offsets = [], []
    early, early_at = [], []
    for piece, source in sources:
        b1 = py(piece, 1)
        b2 = py(piece, -1)
        b3 = py(b1, 1)
        early.append(piece)
        early_at.append(source * rows + y * chunk)
        pieces += [b1, b2, b3]
        offsets += [
            source * rows + (y - sign) % 4 * chunk,
            source * rows + (y + sign) % 4 * chunk,
            source * rows + (y ^ 2) * chunk,
        ]

    place = jnp.arange(BLOCK, dtype=jnp.int32)
    tri = (place[:, None] >= place[None, :]).astype(F32)
    pair = decays.reshape(2, BLOCK, HPC)
    cum = jnp.einsum("ts,bsh->bth", tri, pair, precision=HIGHEST)
    ends = cum[:, -1, :]
    scale = 1.0 / math.sqrt(HALF)
    total = ends[0] + ends[1]
    before = jnp.zeros_like(total)
    gains = [jnp.stack([jnp.zeros_like(cum[0]), scale * jnp.exp(cum[1])])]
    scale_other, scale_mine = [], []
    for bit, mask in zip(range(1, BITS), MASKS):
        upper = (ctx >> bit & 1) > 0
        lead = jnp.stack([before, before + ends[0]])
        gains.append(jnp.where(upper, scale * jnp.exp(cum + lead[:, None, :]), 0.0))
        other = swap(total, mask)
        scale_other.append(jnp.exp(jnp.where(upper, total, 0.0)))
        scale_mine.append(jnp.exp(jnp.where(upper, 0.0, other)))
        before = jnp.where(upper, before + other, before)
        total = total + other
    gl = jnp.concatenate(
        [
            jnp.full((2, BLOCK, HPC, INNER), scale, F32),
            jnp.stack(gains, axis=-1),
            jnp.zeros((2, BLOCK, HPC, LEVELS - INNER - BITS), F32),
        ],
        axis=-1,
    ).reshape(2 * BLOCK, HPC * LEVELS)
    gl = jnp.concatenate(
        [
            jnp.pad(gl[:, :cut], ((0, 0), (0, HALF - cut))),
            jnp.pad(gl[:, cut:], ((0, 0), (0, HALF - (HPC * LEVELS - cut)))),
        ],
        axis=1,
    )
    remain = jnp.exp(ends[:, None, :] - cum).reshape(2 * BLOCK, HPC).T
    high_total = jnp.broadcast_to(jnp.exp(ends[1])[:, None], (HPC, HALF))
    cum = cum.reshape(2 * BLOCK, HPC)
    cum_t = cum.T

    small_at = jnp.stack([x, (x - sign) % n_dp, (x + sign) % n_dp, x ^ 2]) * rows
    q, k, lam = call(
        functools.partial(small_kernel, 4),
        (
            jax.ShapeDtypeStruct((2 * BLOCK, HALF), BF16),
            jax.ShapeDtypeStruct((2 * BLOCK, HALF), BF16),
            jax.ShapeDtypeStruct((2 * BLOCK, 2 * HALF), F32),
        ),
        (small_at, tokens, gl, small, s1, s2, s3),
        smem=1,
        flops=2 * 512 * 4096 * 512,
        nbytes=8 << 20,
    )
    own = lax.dynamic_slice(value_weight, (0, core * half), (rows, half))
    first_at = jnp.stack([x * rows] + early_at)
    first = call(
        functools.partial(value_kernel, 4, True),
        jax.ShapeDtypeStruct((2 * BLOCK, half), F32),
        (first_at, tokens, own, *early),
        smem=1,
        flops=2 * 512 * 1792 * 1024,
        nbytes=8 << 20,
    )
    v = call(
        functools.partial(value_kernel, 9, False),
        jax.ShapeDtypeStruct((2 * BLOCK, half), BF16),
        (jnp.stack(offsets), tokens, first, *pieces),
        smem=1,
        flops=2 * 512 * 2304 * 1024,
        nbytes=12 << 20,
    )

    state, low_state = call(
        state_kernel,
        (
            jax.ShapeDtypeStruct((HALF, half), F32),
            jax.ShapeDtypeStruct((HALF, half), BF16),
        ),
        (k, v, remain, high_total),
        flops=2 * 512 * 128 * 1024,
        nbytes=2 << 20,
    )
    near = call(
        near_kernel,
        jax.ShapeDtypeStruct((2 * BLOCK, half), F32),
        (q, k, v, lam, cum, cum_t, low_state),
        flops=2 * 512 * 512 * 1024,
        nbytes=16 << 20,
    )
    carried = []
    for bit, mask in zip(range(1, BITS), MASKS):
        other = swap(state.astype(BF16), mask)
        carried.append(other)
        if bit + 1 < BITS:
            state = (
                jnp.repeat(scale_other[bit - 1], HALF)[None, :] * other.astype(F32)
                + jnp.repeat(scale_mine[bit - 1], HALF)[None, :] * state
            )
    gain = lax.dynamic_slice(norm_gain, (core * half,), (half,)).reshape(1, half)
    mixed = call(
        functools.partial(far_kernel, (1, 2, 3), False),
        jax.ShapeDtypeStruct((2 * BLOCK, half), F32),
        (q, lam, gain, near, *carried[:3]),
        flops=2 * 512 * 128 * 1024 * 3,
        nbytes=5 << 20,
    )
    out = call(
        functools.partial(far_kernel, (4, 5), True),
        jax.ShapeDtypeStruct((2 * BLOCK, half), BF16),
        (q, lam, gain, mixed, *carried[3:]),
        flops=2 * 512 * 128 * 1024 * 2,
        nbytes=4 << 20,
    )
    keep = lax.dynamic_slice(out, (core * BLOCK, 0), (BLOCK, half))
    give = lax.dynamic_slice(out, ((1 - core) * BLOCK, 0), (BLOCK, half))
    return in_order(keep, swap(give, 1), axis=1)[None]


def solution(mesh):
    return jax.shard_map(
        per_device,
        mesh=mesh,
        in_specs=(
            P("dp", "ctx", None),
            P("dp", None),
            P("dp", None),
            P("dp", None),
            P("dp", None),
            P("dp", "ctx", None),
            P(),
        ),
        out_specs=P("dp", "ctx", None),
        check_vma=False,
    )
```

time: 459 us -> 171 us (0.37)
  waiting for transfers between devices: 350 us -> 43.2 us
  Pallas kernels: 0 us -> 40.9 us
  starting transfers between devices: 22.3 us -> 59.7 us
  matrix products: 34 us -> 0.19 us
  between operations: 13.5 us -> 0.53 us
  other arithmetic: 24.9 us -> 13.1 us
    all_gather x4 -> x0, waiting for transfers between devices: 225 us -> none  [the longest x1 155 us: per_device(): lax.all_gather(value_weight, 'dp', axis=0, tiled=True)]
    ppermute x11 -> x27, waiting for transfers between devices: 123 us -> 43.2 us  [the longest x12 24.7 us: swap(): return lax.ppermute(a, 'ctx', xor_pairs(mask, n_ctx))]
    pallas_call x0 -> x7, Pallas kernels: none -> 40.9 us  [call(): pl.pallas_call(kernel, out_shape=outs, in_specs=specs, out_specs=jax.tree...]
    ppermute x11 -> x27, starting transfers between devices: 22.1 us -> 59.7 us  [the longest x12 39.4 us: swap(): return lax.ppermute(a, 'ctx', xor_pairs(mask, n_ctx))]
    dot_general x8 -> x1, matrix products: 21.5 us -> 0.19 us  [per_device(): cum = jnp.einsum('ts,bsh->bth', tri, pair, precision=HIGHEST)]
    convert_element_type x7 -> x5, other arithmetic: 15.7 us -> 2.78 us  [per_device(): other = swap(state.astype(BF16), mask)]
    unnamed x6 -> x0, matrix products: 12.5 us -> none
    dynamic_slice x0 -> x4, local copies, waits for them, and re-layouts: none -> 6.98 us  [the longest x1 3.36 us: per_device(): own = lax.dynamic_slice(value_weight, (0, core * half), (rows, half))]
  transfers between devices with their start and end apart: 15 -> 27, of which waited for: 14 -> 16; matrix products, arithmetic and copies ran while one was open for 9% -> 9% of each run, Pallas kernels for 0% -> 15%
where the time goes in v1:
time: 171 us; the launch traced here: 170 us
  starting transfers between devices  59.7 us (35%)
  waiting for transfers between devices  43.2 us (25%)
  Pallas kernels  40.9 us (24%)
  other arithmetic  13.1 us (8%)
  local copies, waits for them, and re-layouts  12.5 us (7%)
    pallas_call x7, Pallas kernels, call(): pl.pallas_call(kernel, out_shape=outs, in_specs=specs, out_specs=jax.tree...  40.9 us
    ppermute x12, starting transfers between devices, swap(): return lax.ppermute(a, 'ctx', xor_pairs(mask, n_ctx))  39.4 us
    ppermute x12, waiting for transfers between devices, swap(): return lax.ppermute(a, 'ctx', xor_pairs(mask, n_ctx))  24.7 us
    ppermute x9, starting transfers between devices, py(): return lax.ppermute(a, 'ctx', ring_y(step, n_ctx))  14.2 us
    ppermute x9, waiting for transfers between devices, py(): return lax.ppermute(a, 'ctx', ring_y(step, n_ctx))  11.2 us
    ppermute x6, waiting for transfers between devices, px(): return lax.ppermute(a, ('dp', 'ctx'), ring_x(step, n_dp, n_ctx))  7.29 us
    ppermute x6, starting transfers between devices, px(): return lax.ppermute(a, ('dp', 'ctx'), ring_x(step, n_dp, n_ctx))  6.05 us
    select_n x2, other arithmetic, in_order(): low = jnp.where(core == 0, mine, other)  3.79 us
  transfers between devices with their start and end apart: 27, of which 16 were waited for; matrix products, arithmetic and copies ran while one was open for 9% of the time, Pallas kernels for 15%

profile of v1, /device:TPU:1, one launch (start us, length us, event | category | flops | bytes accessed | tf_op | source)
XLA Modules:
  0.0 170.2 jit_solution(14076717869478279212)
XLA Ops:
  2.0 3.3 %collective-permute-start.9 = (bf16[256,1024]{1,0:T(8,128)(2,1)}, bf16[256,1024]{1,0:T(8,128)(2,1)}, u32[]{:S(2)}, u32[]{:S(2)}) collective-permute-start(bf16[256,1024]{1,0:T(8,128)(2,1)} %dynamic_slice.25), channel_id=1, source_target_pairs={{0,64},{1,193},{2,66},{3,195},{4,68},{5,197},{6,70},{7,199},{8,72}... | collective-permute-start | bytes 1572872 | tf_op jit(solution)/shard_map/ppermute | solution.py:189
  5.3 3.2 %collective-permute-start = (bf16[256,4096]{1,0:T(8,128)(2,1)}, bf16[256,4096]{1,0:T(8,128)(2,1)}, u32[]{:S(2)}, u32[]{:S(2)}) collective-permute-start(bf16[256,4096]{1,0:T(8,128)(2,1)} %bitcast.93), channel_id=1, source_target_pairs={{0,1},{1,0},{2,3},{3,2},{4,5},{5,4},{6,7},{7,6},{8,9},{9,8},{10,11... | collective-permute-start | bytes 6291464 | tf_op jit(solution)/shard_map/ppermute | solution.py:195
  9.2 3.4 %constant_dynamic-slice_fusion.2.refs_0_ = bf16[1024,1024]{1,0:T(8,128)(2,1)} fusion(bf16[1024,2048]{1,0:T(8,128)(2,1)} %param.10, s32[]{:T(128)S(6)} %select_n.210), kind=kLoop, calls=%fused_computation.57 | loop fusion | bytes 4194308 | tf_op jit(solution)/shard_map/dynamic_slice | solution.py:293
  24.6 4.1 %collective-permute-start.5 = (f32[8]{0:T(128)S(1)}, f32[8]{0:T(128)S(1)}, u32[]{:S(2)}, u32[]{:S(2)}) collective-permute-start(f32[8]{0:T(128)S(1)} %get-tuple-element.18), channel_id=1, source_target_pairs={{0,24},{1,25},{2,26},{3,27},{4,28},{5,29},{6,30},{7,31},{8,16},{9,... | collective-permute-start | bytes 104 | tf_op jit(solution)/shard_map/ppermute | solution.py:195
  36.1 3.2 %collective-permute-done.11.refs_3_ = bf16[256,1024]{1,0:T(8,128)(2,1)} collective-permute-done((bf16[256,1024]{1,0:T(8,128)(2,1)}, bf16[256,1024]{1,0:T(8,128)(2,1)}, u32[]{:S(2)}, u32[]{:S(2)}) %collective-permute-start.11) | collective-permute-done | bytes 524320 | tf_op jit(solution)/shard_map/ppermute | solution.py:189
  40.1 3.4 %collective-permute-start.15 = (bf16[256,1024]{1,0:T(8,128)(2,1)}, bf16[256,1024]{1,0:T(8,128)(2,1)S(1)}, u32[]{:S(2)}, u32[]{:S(2)}) collective-permute-start(bf16[256,1024]{1,0:T(8,128)(2,1)} %collective-permute-done.10.refs_2_), channel_id=1, source_target_pairs={{0,2},{1,7},{2,4},{3,1},{4,6},{5,3},{6,0},{7,5},{8,10},{9,15},{10,... | collective-permute-start | bytes 1572872 | tf_op jit(solution)/shard_map/ppermute | solution.py:192
  51.5 3.5 %collective-permute-done.7.refs_2_ = bf16[1024,512]{1,0:T(8,128)(2,1)S(1)} collective-permute-done((bf16[1024,512]{1,0:T(8,128)(2,1)S(1)}, bf16[1024,512]{1,0:T(8,128)(2,1)S(1)}, u32[]{:S(2)}, u32[]{:S(2)}) %collective-permute-start.7) | collective-permute-done | bytes 1048608 | tf_op jit(solution)/shard_map/ppermute | solution.py:189
  57.8 3.3 %collective-permute-start.17 = (bf16[256,1024]{1,0:T(8,128)(2,1)S(1)}, bf16[256,1024]{1,0:T(8,128)(2,1)S(1)}, u32[]{:S(2)}, u32[]{:S(2)}) collective-permute-start(bf16[256,1024]{1,0:T(8,128)(2,1)S(1)} %collective-permute-done.15.refs_4_), channel_id=1, source_target_pairs={{0,2},{1,7},{2,4},{3,1},{4,6},{5,3},{6,0},{7,5},{8,10},{9,15},{10,... | collective-permute-start | bytes 1572872 | tf_op jit(solution)/shard_map/ppermute | solution.py:192
  61.7 2.8 %collective-permute-start.20 = (bf16[256,1024]{1,0:T(8,128)(2,1)S(1)}, bf16[256,1024]{1,0:T(8,128)(2,1)S(1)}, u32[]{:S(2)}, u32[]{:S(2)}) collective-permute-start(bf16[256,1024]{1,0:T(8,128)(2,1)S(1)} %collective-permute-done.18.refs_7_), channel_id=1, source_target_pairs={{0,2},{1,7},{2,4},{3,1},{4,6},{5,3},{6,0},{7,5},{8,10},{9,15},{10,... | collective-permute-start | bytes 1572872 | tf_op jit(solution)/shard_map/ppermute | solution.py:192
  67.0 7.2 %shard_map.74.refs_0_ = f32[512,1024]{1,0:T(8,128)} custom-call(s32[4]{0:T(128)} %pad_add_fusion.off_ref, bf16[512,4096]{1,0:T(8,128)(2,1)} %pad_maximum_fusion.tok_ref, bf16[1024,1024]{1,0:T(8,128)(2,1)} %constant_dynamic-slice_fusion.2.refs_0_, bf16[256,1024]{1,0:T(8,128)(2,1)} %collective-permute-done.9.refs_1_, ...), custom_call_target="tpu_custom_call" | custom-call | flops 1879048192 | bytes 8388608 | tf_op jit(solution)/shard_map/pallas_call | solution.py:53
  74.2 6.9 %shard_map.73 = (bf16[512,128]{1,0:T(8,128)(2,1)}, bf16[512,128]{1,0:T(8,128)(2,1)}, f32[512,256]{1,0:T(8,128)}) custom-call(s32[4]{0:T(128)} %add_multiply_fusion.off_ref, bf16[512,4096]{1,0:T(8,128)(2,1)} %pad_maximum_fusion.tok_ref, f32[512,256]{1,0:T(8,128)} %select_maximum_fusion.gl_ref, bf16[1024,512]{1,0:T(8,128)(2,1)} %copy-done.2, ...), custom_call_target="tpu_custom_call" | custom-call | flops 2147483648 | bytes 8388608 | tf_op jit(solution)/shard_map/pallas_call | solution.py:53
  81.2 5.2 %collective-permute-done.20.refs_9_ = bf16[256,1024]{1,0:T(8,128)(2,1)S(1)} collective-permute-done((bf16[256,1024]{1,0:T(8,128)(2,1)S(1)}, bf16[256,1024]{1,0:T(8,128)(2,1)S(1)}, u32[]{:S(2)}, u32[]{:S(2)}) %collective-permute-start.20) | collective-permute-done | bytes 524320 | tf_op jit(solution)/shard_map/ppermute | solution.py:192
  87.2 8.3 %shard_map.75.v_ref = bf16[512,1024]{1,0:T(8,128)(2,1)} custom-call(s32[9]{0:T(128)} %stack.155.off_ref, bf16[512,4096]{1,0:T(8,128)(2,1)} %pad_maximum_fusion.tok_ref, f32[512,1024]{1,0:T(8,128)} %shard_map.74.refs_0_, bf16[256,1024]{1,0:T(8,128)(2,1)} %collective-permute-done.12.refs_1_, bf16[256,1024]{1,0:T(8,128)(2,1)} %copy-done.10, ...), custom_call_target="tpu_custom_call" | custom-call | flops 2415919104 | bytes 12582912 | tf_op jit(solution)/shard_map/pallas_call | solution.py:53
  100.2 5.1 %collective-permute-done.21.refs_0_ = bf16[128,1024]{1,0:T(8,128)(2,1)S(1)} collective-permute-done((bf16[128,1024]{1,0:T(8,128)(2,1)S(1)}, bf16[128,1024]{1,0:T(8,128)(2,1)S(1)}, u32[]{:S(2)}, u32[]{:S(2)}) %collective-permute-start.21) | collective-permute-done | bytes 262176 | tf_op jit(solution)/shard_map/ppermute | solution.py:195
  106.5 3.5 %collective-permute-start.22 = (bf16[128,1024]{1,0:T(8,128)(2,1)S(1)}, bf16[128,1024]{1,0:T(8,128)(2,1)S(1)}, u32[]{:S(2)}, u32[]{:S(2)}) collective-permute-start(bf16[128,1024]{1,0:T(8,128)(2,1)S(1)} %fusion.2), channel_id=1, source_target_pairs={{0,6},{1,7},{2,4},{3,5},{4,2},{5,3},{6,0},{7,1},{8,14},{9,15},{10,... | collective-permute-start | bytes 786440 | tf_op jit(solution)/shard_map/ppermute | solution.py:195
  110.1 3.6 %collective-permute-done.22.refs_1_ = bf16[128,1024]{1,0:T(8,128)(2,1)S(1)} collective-permute-done((bf16[128,1024]{1,0:T(8,128)(2,1)S(1)}, bf16[128,1024]{1,0:T(8,128)(2,1)S(1)}, u32[]{:S(2)}, u32[]{:S(2)}) %collective-permute-start.22) | collective-permute-done | bytes 262176 | tf_op jit(solution)/shard_map/ppermute | solution.py:195
  114.1 5.1 %collective-permute-done.23.refs_2_ = bf16[128,1024]{1,0:T(8,128)(2,1)S(1)} collective-permute-done((bf16[128,1024]{1,0:T(8,128)(2,1)S(1)}, bf16[128,1024]{1,0:T(8,128)(2,1)S(1)}, u32[]{:S(2)}, u32[]{:S(2)}) %collective-permute-start.23) | collective-permute-done | bytes 262176 | tf_op jit(solution)/shard_map/ppermute | solution.py:195
  119.3 3.0 %collective-permute-start.24 = (bf16[128,1024]{1,0:T(8,128)(2,1)S(1)}, bf16[128,1024]{1,0:T(8,128)(2,1)S(1)}, u32[]{:S(2)}, u32[]{:S(2)}) collective-permute-start(bf16[128,1024]{1,0:T(8,128)(2,1)S(1)} %fusion.3), channel_id=1, source_target_pairs={{0,24},{1,25},{2,26},{3,27},{4,28},{5,29},{6,30},{7,31},{8,16},{9,... | collective-permute-start | bytes 786440 | tf_op jit(solution)/shard_map/ppermute | solution.py:195
  122.5 4.0 %collective-permute-done.24.refs_0_ = bf16[128,1024]{1,0:T(8,128)(2,1)S(1)} collective-permute-done((bf16[128,1024]{1,0:T(8,128)(2,1)S(1)}, bf16[128,1024]{1,0:T(8,128)(2,1)S(1)}, u32[]{:S(2)}, u32[]{:S(2)}) %collective-permute-start.24) | collective-permute-done | bytes 262176 | tf_op jit(solution)/shard_map/ppermute | solution.py:195
  126.7 4.5 %collective-permute-start.25 = (bf16[128,1024]{1,0:T(8,128)(2,1)S(1)}, bf16[128,1024]{1,0:T(8,128)(2,1)S(1)}, u32[]{:S(2)}, u32[]{:S(2)}) collective-permute-start(bf16[128,1024]{1,0:T(8,128)(2,1)S(1)} %add_convert_fusion), channel_id=1, source_target_pairs={{0,56},{1,57},{2,58},{3,59},{4,60},{5,61},{6,62},{7,63},{8,48},{9,... | collective-permute-start | bytes 786440 | tf_op jit(solution)/shard_map/ppermute | solution.py:195
  132.6 5.9 %shard_map.77.base_ref = f32[512,1024]{1,0:T(8,128)} custom-call(bf16[512,128]{1,0:T(8,128)(2,1)} %get-tuple-element.10.q_ref, bf16[512,128]{1,0:T(8,128)(2,1)} %get-tuple-element.12.k_ref, bf16[512,1024]{1,0:T(8,128)(2,1)} %shard_map.75.v_ref, f32[512,256]{1,0:T(8,128)} %get-tuple-element.11.lam_ref, f32[512,8]{1,0:T(8,128)} %copy.25.cum_ref, ...), custom_call_target="tpu_custom_call" | custom-call | flops 536870912 | bytes 16777216 | tf_op jit(solution)/shard_map/pallas_call | solution.py:53
  138.5 5.1 %shard_map.78.base_ref = f32[512,1024]{1,0:T(8,128)} custom-call(bf16[512,128]{1,0:T(8,128)(2,1)} %get-tuple-element.10.q_ref, f32[512,256]{1,0:T(8,128)} %get-tuple-element.11.lam_ref, f32[1,1024]{1,0:T(1,128)} %bitcast.103, f32[512,1024]{1,0:T(8,128)} %shard_map.77.base_ref, bf16[128,1024]{1,0:T(8,128)(2,1)} %copy-done.3, bf16[128,1024]{1,0:T(8,128)(2,1)} %copy-done.8, ...), custom_call_target="tpu_custom_call" | custom-call | flops 402653184 | bytes 5242880 | tf_op jit(solution)/shard_map/pallas_call | solution.py:53
  144.3 5.0 %shard_map.79 = bf16[512,1024]{1,0:T(8,128)(2,1)} custom-call(bf16[512,128]{1,0:T(8,128)(2,1)} %get-tuple-element.10.q_ref, f32[512,256]{1,0:T(8,128)} %get-tuple-element.11.lam_ref, f32[1,1024]{1,0:T(1,128)} %bitcast.104, f32[512,1024]{1,0:T(8,128)} %shard_map.78.base_ref, bf16[128,1024]{1,0:T(8,128)(2,1)} %copy-done.9, bf16[128,1024]{1,0:T(8,128)(2,1)} %copy-done.19), custom_call_target="tpu_custom_call" | custom-call | flops 268435456 | bytes 4194304 | tf_op jit(solution)/shard_map/pallas_call | solution.py:53
  150.4 15.9 %collective-permute-start.26 = (bf16[256,1024]{1,0:T(8,128)(2,1)S(1)}, bf16[256,1024]{1,0:T(8,128)(2,1)S(1)}, u32[]{:S(2)}, u32[]{:S(2)}) collective-permute-start(bf16[256,1024]{1,0:T(8,128)(2,1)S(1)} %constant_dynamic-slice_fusion.1), channel_id=1, source_target_pairs={{0,1},{1,0},{2,3},{3,2},{4,5},{5,4},{6,7},{7,6},{8,9},{9,8},{10,11... | collective-permute-start | bytes 1572872 | tf_op jit(solution)/shard_map/ppermute | solution.py:195
  (151 shorter events, 51.2 us)
Async XLA Ops:
  2.0 28.6 %collective-permute-start.9 = (bf16[256,1024]{1,0:T(8,128)(2,1)}, bf16[256,1024]{1,0:T(8,128)(2,1)}, u32[]{:S(2)}, u32[]{:S(2)}) collective-permute-start(bf16[256,1024]{1,0:T(8,128)(2,1)} %dynamic_slice.25), channel_id=1, source_target_pairs={{0,64},{1,193},{2,66},{3,195},{4,68},{5,197},{6,70},{7,199},{8,72}... | collective-permute-start | bytes 1572872 | tf_op jit(solution)/shard_map/ppermute | solution.py:189
  5.3 29.7 %collective-permute-start.10 = (bf16[256,1024]{1,0:T(8,128)(2,1)}, bf16[256,1024]{1,0:T(8,128)(2,1)}, u32[]{:S(2)}, u32[]{:S(2)}) collective-permute-start(bf16[256,1024]{1,0:T(8,128)(2,1)} %dynamic_slice.25), channel_id=1, source_target_pairs={{0,192},{1,65},{2,194},{3,67},{4,196},{5,69},{6,198},{7,71},{8,200... | collective-permute-start | bytes 1572872 | tf_op jit(solution)/shard_map/ppermute | solution.py:189
  5.3 38.3 %collective-permute-start = (bf16[256,4096]{1,0:T(8,128)(2,1)}, bf16[256,4096]{1,0:T(8,128)(2,1)}, u32[]{:S(2)}, u32[]{:S(2)}) collective-permute-start(bf16[256,4096]{1,0:T(8,128)(2,1)} %bitcast.93), channel_id=1, source_target_pairs={{0,1},{1,0},{2,3},{3,2},{4,5},{5,4},{6,7},{7,6},{8,9},{9,8},{10,11... | collective-permute-start | bytes 6291464 | tf_op jit(solution)/shard_map/ppermute | solution.py:195
  8.5 6.0 %collective-permute-start.1 = (f32[256,16]{0,1:T(8,128)}, f32[256,16]{0,1:T(8,128)S(1)}, u32[]{:S(2)}, u32[]{:S(2)}) collective-permute-start(f32[256,16]{0,1:T(8,128)} %bitcast.106), channel_id=1, source_target_pairs={{0,1},{1,0},{2,3},{3,2},{4,5},{5,4},{6,7},{7,6},{8,9},{9,8},{10,11... | collective-permute-start | bytes 49160 | tf_op jit(solution)/shard_map/ppermute | solution.py:195
  9.1 34.5 %collective-permute-start.6 = (bf16[1024,512]{1,0:T(8,128)(2,1)S(1)}, bf16[1024,512]{1,0:T(8,128)(2,1)S(1)}, u32[]{:S(2)}, u32[]{:S(2)}) collective-permute-start(bf16[1024,512]{1,0:T(8,128)(2,1)S(1)} %fusion.1.refs_0_), channel_id=1, source_target_pairs={{0,64},{1,193},{2,66},{3,195},{4,68},{5,197},{6,70},{7,199},{8,72}... | collective-permute-start | bytes 3145736 | tf_op jit(solution)/shard_map/ppermute | solution.py:189
  24.6 5.1 %collective-permute-start.5 = (f32[8]{0:T(128)S(1)}, f32[8]{0:T(128)S(1)}, u32[]{:S(2)}, u32[]{:S(2)}) collective-permute-start(f32[8]{0:T(128)S(1)} %get-tuple-element.18), channel_id=1, source_target_pairs={{0,24},{1,25},{2,26},{3,27},{4,28},{5,29},{6,30},{7,31},{8,16},{9,... | collective-permute-start | bytes 104 | tf_op jit(solution)/shard_map/ppermute | solution.py:195
  30.6 8.7 %collective-permute-start.11 = (bf16[256,1024]{1,0:T(8,128)(2,1)}, bf16[256,1024]{1,0:T(8,128)(2,1)}, u32[]{:S(2)}, u32[]{:S(2)}) collective-permute-start(bf16[256,1024]{1,0:T(8,128)(2,1)} %collective-permute-done.9.refs_1_), channel_id=1, source_target_pairs={{0,64},{1,193},{2,66},{3,195},{4,68},{5,197},{6,70},{7,199},{8,72}... | collective-permute-start | bytes 1572872 | tf_op jit(solution)/shard_map/ppermute | solution.py:189
  31.0 9.1 %collective-permute-start.12 = (bf16[256,1024]{1,0:T(8,128)(2,1)}, bf16[256,1024]{1,0:T(8,128)(2,1)}, u32[]{:S(2)}, u32[]{:S(2)}) collective-permute-start(bf16[256,1024]{1,0:T(8,128)(2,1)} %collective-permute-done.9.refs_1_), channel_id=1, source_target_pairs={{0,2},{1,7},{2,4},{3,1},{4,6},{5,3},{6,0},{7,5},{8,10},{9,15},{10,... | collective-permute-start | bytes 1572872 | tf_op jit(solution)/shard_map/ppermute | solution.py:192
  35.0 20.0 %collective-permute-start.7 = (bf16[1024,512]{1,0:T(8,128)(2,1)S(1)}, bf16[1024,512]{1,0:T(8,128)(2,1)S(1)}, u32[]{:S(2)}, u32[]{:S(2)}) collective-permute-start(bf16[1024,512]{1,0:T(8,128)(2,1)S(1)} %fusion.1.refs_0_), channel_id=1, source_target_pairs={{0,192},{1,65},{2,194},{3,67},{4,196},{5,69},{6,198},{7,71},{8,200... | collective-permute-start | bytes 3145736 | tf_op jit(solution)/shard_map/ppermute | solution.py:189
  39.3 10.7 %collective-permute-start.13 = (bf16[256,1024]{1,0:T(8,128)(2,1)}, bf16[256,1024]{1,0:T(8,128)(2,1)S(1)}, u32[]{:S(2)}, u32[]{:S(2)}) collective-permute-start(bf16[256,1024]{1,0:T(8,128)(2,1)} %collective-permute-done.9.refs_1_), channel_id=1, source_target_pairs={{0,6},{1,3},{2,0},{3,5},{4,2},{5,7},{6,4},{7,1},{8,14},{9,11},{10,... | collective-permute-start | bytes 1572872 | tf_op jit(solution)/shard_map/ppermute | solution.py:192
  40.1 9.9 %collective-permute-start.15 = (bf16[256,1024]{1,0:T(8,128)(2,1)}, bf16[256,1024]{1,0:T(8,128)(2,1)S(1)}, u32[]{:S(2)}, u32[]{:S(2)}) collective-permute-start(bf16[256,1024]{1,0:T(8,128)(2,1)} %collective-permute-done.10.refs_2_), channel_id=1, source_target_pairs={{0,2},{1,7},{2,4},{3,1},{4,6},{5,3},{6,0},{7,5},{8,10},{9,15},{10,... | collective-permute-start | bytes 1572872 | tf_op jit(solution)/shard_map/ppermute | solution.py:192
  43.6 14.3 %collective-permute-start.18 = (bf16[256,1024]{1,0:T(8,128)(2,1)}, bf16[256,1024]{1,0:T(8,128)(2,1)S(1)}, u32[]{:S(2)}, u32[]{:S(2)}) collective-permute-start(bf16[256,1024]{1,0:T(8,128)(2,1)} %collective-permute-done.11.refs_3_), channel_id=1, source_target_pairs={{0,2},{1,7},{2,4},{3,1},{4,6},{5,3},{6,0},{7,5},{8,10},{9,15},{10,... | collective-permute-start | bytes 1572872 | tf_op jit(solution)/shard_map/ppermute | solution.py:192
  43.6 18.1 %collective-permute-start.8 = (bf16[1024,512]{1,0:T(8,128)(2,1)S(1)}, bf16[1024,512]{1,0:T(8,128)(2,1)S(1)}, u32[]{:S(2)}, u32[]{:S(2)}) collective-permute-start(bf16[1024,512]{1,0:T(8,128)(2,1)S(1)} %collective-permute-done.6.refs_1_), channel_id=1, source_target_pairs={{0,64},{1,193},{2,66},{3,195},{4,68},{5,197},{6,70},{7,199},{8,72}... | collective-permute-start | bytes 3145736 | tf_op jit(solution)/shard_map/ppermute | solution.py:189
  50.0 31.1 %collective-permute-start.16 = (bf16[256,1024]{1,0:T(8,128)(2,1)}, bf16[256,1024]{1,0:T(8,128)(2,1)S(1)}, u32[]{:S(2)}, u32[]{:S(2)}) collective-permute-start(bf16[256,1024]{1,0:T(8,128)(2,1)} %collective-permute-done.10.refs_2_), channel_id=1, source_target_pairs={{0,6},{1,3},{2,0},{3,5},{4,2},{5,7},{6,4},{7,1},{8,14},{9,11},{10,... | collective-permute-start | bytes 1572872 | tf_op jit(solution)/shard_map/ppermute | solution.py:192
  50.0 31.1 %collective-permute-start.19 = (bf16[256,1024]{1,0:T(8,128)(2,1)}, bf16[256,1024]{1,0:T(8,128)(2,1)S(1)}, u32[]{:S(2)}, u32[]{:S(2)}) collective-permute-start(bf16[256,1024]{1,0:T(8,128)(2,1)} %collective-permute-done.11.refs_3_), channel_id=1, source_target_pairs={{0,6},{1,3},{2,0},{3,5},{4,2},{5,7},{6,4},{7,1},{8,14},{9,11},{10,... | collective-permute-start | bytes 1572872 | tf_op jit(solution)/shard_map/ppermute | solution.py:192
  55.0 26.1 %collective-permute-start.14 = (bf16[256,1024]{1,0:T(8,128)(2,1)}, bf16[256,1024]{1,0:T(8,128)(2,1)S(1)}, u32[]{:S(2)}, u32[]{:S(2)}) collective-permute-start(bf16[256,1024]{1,0:T(8,128)(2,1)} %collective-permute-done.12.refs_1_), channel_id=1, source_target_pairs={{0,2},{1,7},{2,4},{3,1},{4,6},{5,3},{6,0},{7,5},{8,10},{9,15},{10,... | collective-permute-start | bytes 1572872 | tf_op jit(solution)/shard_map/ppermute | solution.py:192
  57.8 23.3 %collective-permute-start.17 = (bf16[256,1024]{1,0:T(8,128)(2,1)S(1)}, bf16[256,1024]{1,0:T(8,128)(2,1)S(1)}, u32[]{:S(2)}, u32[]{:S(2)}) collective-permute-start(bf16[256,1024]{1,0:T(8,128)(2,1)S(1)} %collective-permute-done.15.refs_4_), channel_id=1, source_target_pairs={{0,2},{1,7},{2,4},{3,1},{4,6},{5,3},{6,0},{7,5},{8,10},{9,15},{10,... | collective-permute-start | bytes 1572872 | tf_op jit(solution)/shard_map/ppermute | solution.py:192
  61.7 24.7 %collective-permute-start.20 = (bf16[256,1024]{1,0:T(8,128)(2,1)S(1)}, bf16[256,1024]{1,0:T(8,128)(2,1)S(1)}, u32[]{:S(2)}, u32[]{:S(2)}) collective-permute-start(bf16[256,1024]{1,0:T(8,128)(2,1)S(1)} %collective-permute-done.18.refs_7_), channel_id=1, source_target_pairs={{0,2},{1,7},{2,4},{3,1},{4,6},{5,3},{6,0},{7,5},{8,10},{9,15},{10,... | collective-permute-start | bytes 1572872 | tf_op jit(solution)/shard_map/ppermute | solution.py:192
  99.9 5.3 %collective-permute-start.21 = (bf16[128,1024]{1,0:T(8,128)(2,1)S(1)}, bf16[128,1024]{1,0:T(8,128)(2,1)S(1)}, u32[]{:S(2)}, u32[]{:S(2)}) collective-permute-start(bf16[128,1024]{1,0:T(8,128)(2,1)S(1)} %convert_element_type.36), channel_id=1, source_target_pairs={{0,2},{1,3},{2,0},{3,1},{4,6},{5,7},{6,4},{7,5},{8,10},{9,11},{10,... | collective-permute-start | bytes 786440 | tf_op jit(solution)/shard_map/ppermute | solution.py:195
  106.5 7.3 %collective-permute-start.22 = (bf16[128,1024]{1,0:T(8,128)(2,1)S(1)}, bf16[128,1024]{1,0:T(8,128)(2,1)S(1)}, u32[]{:S(2)}, u32[]{:S(2)}) collective-permute-start(bf16[128,1024]{1,0:T(8,128)(2,1)S(1)} %fusion.2), channel_id=1, source_target_pairs={{0,6},{1,7},{2,4},{3,5},{4,2},{5,3},{6,0},{7,1},{8,14},{9,15},{10,... | collective-permute-start | bytes 786440 | tf_op jit(solution)/shard_map/ppermute | solution.py:195
  113.9 5.3 %collective-permute-start.23 = (bf16[128,1024]{1,0:T(8,128)(2,1)S(1)}, bf16[128,1024]{1,0:T(8,128)(2,1)S(1)}, u32[]{:S(2)}, u32[]{:S(2)}) collective-permute-start(bf16[128,1024]{1,0:T(8,128)(2,1)S(1)} %get-tuple-element.21), channel_id=1, source_target_pairs={{0,8},{1,9},{2,10},{3,11},{4,12},{5,13},{6,14},{7,15},{8,0},{9,1},... | collective-permute-start | bytes 786440 | tf_op jit(solution)/shard_map/ppermute | solution.py:195
  119.3 7.2 %collective-permute-start.24 = (bf16[128,1024]{1,0:T(8,128)(2,1)S(1)}, bf16[128,1024]{1,0:T(8,128)(2,1)S(1)}, u32[]{:S(2)}, u32[]{:S(2)}) collective-permute-start(bf16[128,1024]{1,0:T(8,128)(2,1)S(1)} %fusion.3), channel_id=1, source_target_pairs={{0,24},{1,25},{2,26},{3,27},{4,28},{5,29},{6,30},{7,31},{8,16},{9,... | collective-permute-start | bytes 786440 | tf_op jit(solution)/shard_map/ppermute | solution.py:195
  126.7 16.9 %collective-permute-start.25 = (bf16[128,1024]{1,0:T(8,128)(2,1)S(1)}, bf16[128,1024]{1,0:T(8,128)(2,1)S(1)}, u32[]{:S(2)}, u32[]{:S(2)}) collective-permute-start(bf16[128,1024]{1,0:T(8,128)(2,1)S(1)} %add_convert_fusion), channel_id=1, source_target_pairs={{0,56},{1,57},{2,58},{3,59},{4,60},{5,61},{6,62},{7,63},{8,48},{9,... | collective-permute-start | bytes 786440 | tf_op jit(solution)/shard_map/ppermute | solution.py:195
  150.4 17.5 %collective-permute-start.26 = (bf16[256,1024]{1,0:T(8,128)(2,1)S(1)}, bf16[256,1024]{1,0:T(8,128)(2,1)S(1)}, u32[]{:S(2)}, u32[]{:S(2)}) collective-permute-start(bf16[256,1024]{1,0:T(8,128)(2,1)S(1)} %constant_dynamic-slice_fusion.1), channel_id=1, source_target_pairs={{0,1},{1,0},{2,3},{3,2},{4,5},{5,4},{6,7},{7,6},{8,9},{9,8},{10,11... | collective-permute-start | bytes 1572872 | tf_op jit(solution)/shard_map/ppermute | solution.py:195
  (28 other events, 381.4 us)

commit v2 on v0

v2 whole, which is shorter than its diff:
```python
import functools
import math

import jax
import jax.numpy as jnp
from jax import lax
from jax.experimental import pallas as pl
from jax.experimental.pallas import tpu as pltpu
from jax.sharding import PartitionSpec as P

HIGHEST = lax.Precision.HIGHEST
F32 = jnp.float32
BF16 = jnp.bfloat16
BLOCK = 256
HALF = 128
LEVELS = 20
INNER = 9
BITS = 6
HPC = 4
MASKS = (6, 8, 24, 56)
BIG = 56
FINISH = BIG
EXTRA = 16


def ring_x(step, n_dp, n_ctx):
    pairs = []
    for x in range(n_dp):
        for c in range(n_ctx):
            to = (x + (step if c % 2 == 0 else -step)) % n_dp
            pairs.append((x * n_ctx + c, to * n_ctx + c))
    return pairs


def xor_pairs(mask, n_ctx):
    return [(c, c ^ mask) for c in range(n_ctx)]


def whole(n):
    return [pl.BlockSpec(memory_space=pltpu.VMEM)] * n


def call(kernel, outs, args, smem=0, flops=0, nbytes=0, mib=16):
    specs = [pl.BlockSpec(memory_space=pltpu.SMEM)] * smem + whole(len(args) - smem)
    return pl.pallas_call(
        kernel,
        out_shape=outs,
        in_specs=specs,
        out_specs=jax.tree.map(lambda _: pl.BlockSpec(memory_space=pltpu.VMEM), outs),
        compiler_params=pltpu.CompilerParams(vmem_limit_bytes=mib << 20),
        cost_estimate=pl.CostEstimate(flops=flops, bytes_accessed=nbytes, transcendentals=0),
    )(*args)


def exact(a, b, contract):
    return lax.dot_general(
        a, b, ((contract[:1], contract[1:]), ((), ())), precision=HIGHEST, preferred_element_type=F32
    )


def prep_kernel(at_ref, mine_ref, other_ref, cum_ref, cumt_ref, remain_ref, logs_ref, gl_ref):
    first = at_ref[0] == 0

    def ours_of(ref):
        rows = ref[:HPC, :]
        for i in range(1, 4):
            rows = jnp.where(at_ref[1] == i, ref[i * HPC : (i + 1) * HPC, :], rows)
        return rows

    mine, other = ours_of(mine_ref), ours_of(other_ref)
    row = lax.broadcasted_iota(jnp.int32, (BLOCK, BLOCK), 0)
    col = lax.broadcasted_iota(jnp.int32, (BLOCK, BLOCK), 1)
    tri = (row >= col).astype(F32)
    scale = 1.0 / math.sqrt(HALF)
    head = lax.broadcasted_iota(jnp.int32, (HPC, HALF), 0)
    lane = lax.broadcasted_iota(jnp.int32, (HPC, HALF), 1)
    local = lane * 3277 >> 16
    level = lane - local * LEVELS
    later_at = ((local == head) & (level > INNER) & (level < INNER + BITS)).astype(F32)
    first_at = ((local == head) & (level == INNER)).astype(F32)
    near_at = jnp.where(level[:1] < INNER, scale, 0.0)
    wide_row = lax.broadcasted_iota(jnp.int32, (HPC, HPC * HALF), 0)
    wide_col = lax.broadcasted_iota(jnp.int32, (HPC, HPC * HALF), 1)
    spread = (wide_col >> 7 == wide_row).astype(F32)
    lead = None
    for b in range(2):
        decay = jnp.where(first, mine, other) if b == 0 else jnp.where(first, other, mine)
        rows = slice(b * BLOCK, (b + 1) * BLOCK)
        across = exact(decay, tri, (1, 1))
        down = exact(tri, decay, (1, 1))
        cumt_ref[:, rows] = across
        remain_ref[:, rows] = jnp.exp(across[:, BLOCK - 1 :] - across)
        cum_ref[rows, :] = down
        end = down[BLOCK - 1 :, :]
        logs_ref[b : b + 1, :] = exact(jnp.broadcast_to(end, (HPC, HPC)), spread, (1, 0))[:1]
        growth = jnp.exp(down) * scale
        if b == 0:
            gl = exact(growth, later_at, (1, 0))
        else:
            later = jnp.exp(down + lead) * scale
            gl = exact(later, later_at, (1, 0)) + exact(growth, first_at, (1, 0))
        gl_ref[rows, :] = gl + near_at
        lead = end


def small_kernel(n, off_ref, mine_ref, other_ref, gl_ref, *refs):
    pieces, (row_ref, lam_ref) = refs[:n], refs[n:]
    for i, tok_ref in enumerate((mine_ref, other_ref)):
        rows = pl.ds(pl.multiple_of((off_ref[n] ^ i) * BLOCK, BLOCK), BLOCK)
        total = None
        for p in range(n):
            depth = pieces[p].shape[0]
            columns = pl.ds(pl.multiple_of(off_ref[p], BLOCK), depth)
            part = jnp.dot(tok_ref[:, columns], pieces[p][...], preferred_element_type=F32)
            total = part if total is None else total + part
        row_ref[rows, :] = total[:, :HALF].astype(BF16)
        lam = total[:, HALF:]
        soft = jnp.maximum(lam, 0.0) + jnp.log1p(jnp.exp(-jnp.abs(lam)))
        lam_ref[rows, :] = soft * gl_ref[rows, :]


def value_kernel(n, first, off_ref, mine_ref, other_ref, *refs):
    refs = list(refs)
    out_ref = refs.pop()
    base = None if first else refs.pop(0)
    for i, tok_ref in enumerate((mine_ref, other_ref)):
        rows = pl.ds(pl.multiple_of((off_ref[n] ^ i) * BLOCK, BLOCK), BLOCK)
        for start in range(0, out_ref.shape[1], BLOCK):
            cols = slice(start, start + BLOCK)
            total = None if first else base[rows, cols]
            for p in range(n):
                depth = refs[p].shape[0]
                columns = pl.ds(pl.multiple_of(off_ref[p], BLOCK), depth)
                part = jnp.dot(tok_ref[:, columns], refs[p][:, cols], preferred_element_type=F32)
                total = part if total is None else total + part
            out_ref[rows, cols] = total.astype(out_ref.dtype)


def put_payload(out_ref, state, log):
    out_ref[:HALF, :] = state.astype(BF16)
    rest = log
    parts = []
    for _ in range(3):
        part = rest.astype(BF16)
        rest = rest - part.astype(F32)
        parts.append(part.astype(F32))
    place = lax.broadcasted_iota(jnp.int32, (EXTRA, log.shape[1]), 0)
    tail = jnp.zeros((EXTRA, log.shape[1]), F32)
    for i, part in enumerate(parts):
        tail = jnp.where(place == i, part, tail)
    out_ref[HALF:, :] = tail.astype(BF16)


def take_payload(ref):
    tail = ref[HALF:, :].astype(F32)
    return ref[:HALF, :].astype(F32), tail[0:1, :] + tail[1:2, :] + tail[2:3, :]


def state_kernel(k_ref, v_ref, remain_ref, logs_ref, low_ref, send_ref):
    kt = jnp.transpose(k_ref[...].astype(F32))
    parts = []
    for h in range(HPC):
        cols = slice(h * HALF, (h + 1) * HALF)
        keyed = (kt * remain_ref[h : h + 1, :]).astype(BF16)
        low = jnp.dot(keyed[:, :BLOCK], v_ref[:BLOCK, cols], preferred_element_type=F32)
        high = jnp.dot(keyed[:, BLOCK:], v_ref[BLOCK:, cols], preferred_element_type=F32)
        low_ref[:, cols] = low.astype(BF16)
        parts.append(jnp.exp(logs_ref[1:2, cols]) * low + high)
    put_payload(send_ref, jnp.concatenate(parts, axis=1), logs_ref[0:1, :] + logs_ref[1:2, :])


def join_kernel(bit, at_ref, mine_ref, got_ref, out_ref):
    upper = (at_ref[0] >> bit & 1) > 0
    (s, log), (t, log_t) = take_payload(mine_ref), take_payload(got_ref)
    a = jnp.exp(jnp.where(upper, log, 0.0))
    b = jnp.exp(jnp.where(upper, 0.0, log_t))
    put_payload(out_ref, a * t + b * s, log + log_t)


def near_kernel(q_ref, k_ref, v_ref, lam_ref, cum_ref, cumt_ref, low_ref, out_ref):
    row = lax.broadcasted_iota(jnp.int32, (HALF, HALF), 0)
    col = lax.broadcasted_iota(jnp.int32, (HALF, HALF), 1)
    differ = jnp.bitwise_xor(row, col)
    level = jnp.zeros((HALF, HALF), jnp.int32)
    for power in range(7):
        level = level + jnp.where(differ >= 1 << power, 1, 0)
    causal = row >= col
    for b in range(2):
        r0 = b * BLOCK
        tiles = [slice(r0, r0 + HALF), slice(r0 + HALF, r0 + BLOCK)]
        scores = lax.dot_general(
            q_ref[r0 : r0 + BLOCK, :],
            k_ref[r0 : r0 + BLOCK, :],
            (((1,), (1,)), ((), ())),
            preferred_element_type=F32,
        )
        s00, s10, s11 = scores[:HALF, :HALF], scores[HALF:, :HALF], scores[HALF:, HALF:]
        for h in range(HPC):
            cols = slice(h * HALF, (h + 1) * HALF)
            inner = h * LEVELS
            lam0 = lam_ref[tiles[0], :]
            lam1 = lam_ref[tiles[1], :]
            index = level + inner
            w00 = jnp.take_along_axis(lam0, index, axis=1)
            w11 = jnp.take_along_axis(lam1, index, axis=1)
            w10 = jnp.broadcast_to(lam1[:, inner + 8 : inner + 9], (HALF, HALF))
            t0 = cum_ref[tiles[0], h : h + 1]
            t1 = cum_ref[tiles[1], h : h + 1]
            c0 = cumt_ref[h : h + 1, tiles[0]]
            c1 = cumt_ref[h : h + 1, tiles[1]]
            m00 = w00 * jnp.exp(jnp.where(causal, t0 - c0, -jnp.inf)) * s00
            m11 = w11 * jnp.exp(jnp.where(causal, t1 - c1, -jnp.inf)) * s11
            m10 = w10 * jnp.exp(t1 - c0) * s10
            v0 = v_ref[tiles[0], cols]
            out0 = jnp.dot(m00.astype(BF16), v0, preferred_element_type=F32)
            mix1 = jnp.concatenate([m10.astype(BF16), m11.astype(BF16)], axis=1)
            out1 = jnp.dot(mix1, v_ref[r0 : r0 + BLOCK, cols], preferred_element_type=F32)
            if b == 1:
                reach = jnp.dot(
                    q_ref[BLOCK:, :], low_ref[:, cols], preferred_element_type=F32
                )
                out0 = out0 + lam0[:, inner + INNER : inner + INNER + 1] * reach[:HALF]
                out1 = out1 + lam1[:, inner + INNER : inner + INNER + 1] * reach[HALF:]
            out_ref[tiles[0], cols] = out0
            out_ref[tiles[1], cols] = out1


def far_kernel(first, bits, outs, at_ref, q_ref, lam_ref, gain_ref, base_ref, *refs):
    n = len(refs) - outs
    got, out_refs = refs[:n], refs[n:]
    last = bits == BITS
    before = jnp.zeros((1, base_ref.shape[1]), F32)
    scales = []
    for i, ref in enumerate(got):
        upper = (at_ref[0] >> i & 1) > 0
        tail = ref[HALF:, :].astype(F32)
        scales.append(jnp.where(upper, jnp.exp(before), 0.0))
        before = before + jnp.where(upper, tail[0:1, :] + tail[1:2, :] + tail[2:3, :], 0.0)
    for pair in range(HPC // 2):
        both = slice(pair * BLOCK, (pair + 1) * BLOCK)
        carried = [
            (scales[bit - 1][:, both] * got[bit - 1][:HALF, both].astype(F32)).astype(BF16)
            for bit in range(first, bits)
        ]
        for o, out_ref in enumerate(out_refs):
            rows = pl.ds(pl.multiple_of(at_ref[1 + o], BLOCK), out_ref.shape[0])
            q, lam = q_ref[rows, :], lam_ref[rows, :]
            reach = [jnp.dot(q, c, preferred_element_type=F32) for c in carried]
            for i in range(2):
                cols = slice(pair * BLOCK + i * HALF, pair * BLOCK + (i + 1) * HALF)
                total = base_ref[rows, cols]
                for bit, part in zip(range(first, bits), reach):
                    slot = (2 * pair + i) * LEVELS + INNER + bit
                    total = total + lam[:, slot : slot + 1] * part[:, i * HALF : (i + 1) * HALF]
                if last:
                    mean = jnp.mean(total * total, axis=1, keepdims=True)
                    total = total * lax.rsqrt(mean + 1e-05) * gain_ref[:, cols]
                out_ref[:, cols] = total.astype(out_ref.dtype)


def place_kernel(at_ref, *refs):
    out_ref, width = refs[-1], refs[0].shape[1]
    for d, ref in enumerate(refs[:-1]):
        out_ref[:, pl.ds(pl.multiple_of((at_ref[0] ^ d) * width, width), width)] = ref[...]


def per_device(inputs, query_weight, key_weight, value_weight, lambda_weight, log_decay, norm_gain):
    n_dp, n_ctx = lax.axis_size("dp"), lax.axis_size("ctx")
    x, ctx = lax.axis_index("dp"), lax.axis_index("ctx")
    core, y0, y1 = ctx & 1, ctx >> 1 & 1, ctx >> 2 & 1
    sign = 1 - 2 * core
    quarter = core + 2 * (y0 ^ y1)
    rows = query_weight.shape[0]
    wide = value_weight.shape[1] // 4

    def px(a):
        return lax.ppermute(a, ("dp", "ctx"), ring_x(1, n_dp, n_ctx))

    def swap(a, mask):
        return lax.ppermute(a, "ctx", xor_pairs(mask, n_ctx))

    def after(a, *done):
        return lax.optimization_barrier((a, *done))[0]

    def shape(r, c, t):
        return jax.ShapeDtypeStruct((r, c), t)

    mine = inputs[0]
    decay_mine = log_decay[0].T
    decay_sib, decay_far, decay_farsib = [swap(decay_mine, m) for m in (1, 2, 3)]
    far = swap(after(mine, decay_far, decay_farsib), 2)
    weights_v = [lax.dynamic_slice(value_weight, (0, quarter * wide), (rows, wide))]
    weights_s = [
        jnp.concatenate(
            [
                jnp.where(core == 0, query_weight, key_weight),
                jnp.pad(
                    lax.dynamic_slice(lambda_weight, (0, quarter * HPC * LEVELS), (rows, HPC * LEVELS)),
                    ((0, 0), (0, HALF - HPC * LEVELS)),
                ),
            ],
            axis=1,
        )
    ]
    weights_s.append(px(weights_s[0]))
    weights_v.append(px(weights_v[0]))
    sib = swap(mine, 1)
    preps = []
    for pair in ((decay_mine, decay_sib), (decay_far, decay_farsib)):
        preps.append(
            call(
                prep_kernel,
                (
                    shape(2 * BLOCK, HPC, F32),
                    shape(HPC, 2 * BLOCK, F32),
                    shape(HPC, 2 * BLOCK, F32),
                    shape(2, wide, F32),
                    shape(2 * BLOCK, HALF, F32),
                ),
                (jnp.stack([core, quarter]), *pair),
                smem=1,
                flops=1 << 24,
                nbytes=1 << 20,
                mib=8,
            )
        )
    weights_s.append(px(weights_s[1]))
    weights_s.append(px(after(weights_s[2], preps[0][4], preps[1][4], sib)))
    weights_v.append(px(after(weights_v[1], weights_s[3])))
    weights_v.append(px(weights_v[2]))
    far = after(far, weights_v[2])
    far_sib = swap(far, 1)
    offsets = jnp.stack([(x - sign * i) % n_dp * rows for i in range(4)] + [core])

    chips = []
    for late in range(2):
        toks = (far, far_sib) if late else (mine, sib)
        cum, cum_t, remain, logs, gl = preps[late]
        made, lam = call(
            functools.partial(small_kernel, 4),
            (shape(2 * BLOCK, HALF, BF16), shape(2 * BLOCK, HALF, F32)),
            (offsets, *toks, gl, *weights_s),
            smem=1,
            flops=2 * 512 * 4096 * 256,
            nbytes=8 << 20,
        )
        fetched = swap(made, 1)
        q = jnp.where(core == 0, made, fetched)
        k = jnp.where(core == 0, fetched, made)
        part = call(
            functools.partial(value_kernel, 3, True),
            shape(2 * BLOCK, wide, F32),
            (jnp.concatenate([offsets[:3], offsets[4:]]), *toks, *weights_v[:3]),
            smem=1,
            flops=2 * 512 * 3072 * wide,
            nbytes=8 << 20,
        )
        chips.append([q, k, lam, part])

    last_v, *parts = lax.optimization_barrier((weights_v[3], chips[0][3], chips[1][3], chips[0][1], chips[1][1]))
    for late in range(2):
        toks = (far, far_sib) if late else (mine, sib)
        cum, cum_t, remain, logs, gl = preps[late]
        q, k, lam, _ = chips[late]
        k = parts[2 + late]
        v = call(
            functools.partial(value_kernel, 1, False),
            shape(2 * BLOCK, wide, BF16),
            (offsets[3:], *toks, parts[late], last_v),
            smem=1,
            flops=2 * 512 * 1024 * wide,
            nbytes=4 << 20,
        )
        payload = shape(HALF + EXTRA, wide, BF16)
        low_state, send = call(
            state_kernel,
            (shape(HALF, wide, BF16), payload),
            (k, v, remain, logs),
            flops=2 * 512 * 128 * wide,
            nbytes=1 << 20,
            mib=8,
        )
        near = call(
            near_kernel,
            shape(2 * BLOCK, wide, F32),
            (q, k, v, lam, cum, cum_t, low_state),
            flops=2 * 512 * 512 * wide,
            nbytes=8 << 20,
            mib=BIG,
        )
        chips[late] = [q, lam, near, send]

    at = ctx >> 1

    def join(bit, mine, got):
        return call(
            functools.partial(join_kernel, bit),
            payload,
            (at.reshape(1), mine, got),
            smem=1,
            flops=1 << 20,
            nbytes=1 << 20,
            mib=8,
        )

    send = join(0, chips[0][3], chips[1][3])
    got = []
    for i, mask in enumerate(MASKS):
        got.append(swap(send, mask))
        if i < 2:
            got[i], chips[1 - i][2] = lax.optimization_barrier((got[i], chips[1 - i][2]))
        if i + 1 < len(MASKS):
            send = join(i + 1, send, got[i])
    gain = lax.dynamic_slice(norm_gain, (quarter * wide,), (wide,)).reshape(1, wide)
    for late in range(2):
        q, lam, near, _ = chips[late]
        chips[late][2] = call(
            functools.partial(far_kernel, 1, 4, 1),
            shape(2 * BLOCK, wide, F32),
            (jnp.stack([at ^ late, 0 * at]), q, lam, gain, near, chips[1 - late][3], *got[:2]),
            smem=1,
            flops=2 * 512 * 128 * wide * 3,
            nbytes=4 << 20,
            mib=BIG,
        )
    got[3], chips[0][2], chips[1][2] = lax.optimization_barrier((got[3], chips[0][2], chips[1][2]))

    def finish(late):
        q, lam, mixed, _ = chips[late]
        return call(
            functools.partial(far_kernel, 4, BITS, 2),
            (shape(BLOCK, wide, BF16),) * 2,
            (
                jnp.stack([at ^ late, core * BLOCK, (1 - core) * BLOCK]),
                q, lam, gain, mixed, chips[1 - late][3], *got,
            ),
            smem=1,
            flops=2 * 512 * 128 * wide * 2,
            nbytes=4 << 20,
            mib=FINISH,
        )

    over, across = finish(1)
    over, across = swap(over, 2), swap(across, 3)
    keep, beside = finish(0)
    beside = swap(beside, 1)
    out = call(
        place_kernel,
        shape(BLOCK, 4 * wide, BF16),
        (quarter.reshape(1), keep, beside, over, across),
        smem=1,
        nbytes=2 << 20,
        mib=8,
    )
    return out[None]


def solution(mesh):
    return jax.shard_map(
        per_device,
        mesh=mesh,
        in_specs=(
            P("dp", "ctx", None),
            P("dp", None),
            P("dp", None),
            P("dp", None),
            P("dp", None),
            P("dp", "ctx", None),
            P(),
        ),
        out_specs=P("dp", "ctx", None),
        check_vma=False,
    )
```

time: 459 us -> 149 us (0.32)
  waiting for transfers between devices: 350 us -> 39.7 us
  Pallas kernels: 0 us -> 49.1 us
  matrix products: 34 us -> 0 us
  other arithmetic: 24.9 us -> 5.36 us
  starting transfers between devices: 22.3 us -> 35.8 us
  between operations: 13.5 us -> 0.44 us
    all_gather x4 -> x0, waiting for transfers between devices: 225 us -> none  [the longest x1 155 us: per_device(): lax.all_gather(value_weight, 'dp', axis=0, tiled=True)]
    ppermute x11 -> x21, waiting for transfers between devices: 123 us -> 39.7 us  [the longest x15 27.6 us: swap(): return lax.ppermute(a, 'ctx', xor_pairs(mask, n_ctx))]
    pallas_call x0 -> x21, Pallas kernels: none -> 49.1 us  [call(): pl.pallas_call(kernel, out_shape=outs, in_specs=specs, out_specs=jax.tree...]
    dot_general x8 -> x0, matrix products: 21.5 us -> none  [the longest x4 14.8 us: accumulate(): jnp.dot(tokens, piece, preferred_element_type=jnp.float32)]
    convert_element_type x7 -> x0, other arithmetic: 15.7 us -> none  [the longest x6 15.4 us: per_device(): carried = (carry_decay[:, None, None] * other_state).astype(jnp.bfloat16)]
    ppermute x11 -> x21, starting transfers between devices: 22.1 us -> 35.8 us  [the longest x15 27.9 us: swap(): return lax.ppermute(a, 'ctx', xor_pairs(mask, n_ctx))]
    unnamed x6 -> x0, matrix products: 12.5 us -> none
    unnamed x61 -> x87, local copies, waits for them, and re-layouts: 4.46 us -> 15.1 us
  transfers between devices with their start and end apart: 15 -> 21, of which waited for: 14 -> 7; matrix products, arithmetic and copies ran while one was open for 9% -> 6% of each run, Pallas kernels for 0% -> 25%
where the time goes in v2:
time: 149 us
  Pallas kernels  49.1 us (33%)
  waiting for transfers between devices  39.7 us (27%)
  starting transfers between devices  35.8 us (24%)
  local copies, waits for them, and re-layouts  18.4 us (12%)
  other arithmetic  5.36 us (4%)
    pallas_call x21, Pallas kernels, call(): pl.pallas_call(kernel, out_shape=outs, in_specs=specs, out_specs=jax.tree...  49.1 us
    ppermute x15, starting transfers between devices, swap(): return lax.ppermute(a, 'ctx', xor_pairs(mask, n_ctx))  27.9 us
    ppermute x15, waiting for transfers between devices, swap(): return lax.ppermute(a, 'ctx', xor_pairs(mask, n_ctx))  27.6 us
    unnamed x87, local copies, waits for them, and re-layouts  15.1 us
    ppermute x6, waiting for transfers between devices, px(): return lax.ppermute(a, ('dp', 'ctx'), ring_x(1, n_dp, n_ctx))  12 us
    ppermute x6, starting transfers between devices, px(): return lax.ppermute(a, ('dp', 'ctx'), ring_x(1, n_dp, n_ctx))  7.97 us
  transfers between devices with their start and end apart: 21, of which 7 were waited for; matrix products, arithmetic and copies ran while one was open for 6% of the time, Pallas kernels for 25%

profile of v2, /device:TPU:1, one launch (start us, length us, event | category | flops | bytes accessed | tf_op | source)
XLA Modules:
  0.0 148.8 jit_solution(10696474932696404935)
XLA Ops:
  0.0 3.2 %collective-permute-start = (bf16[256,4096]{1,0:T(8,128)(2,1)}, bf16[256,4096]{1,0:T(8,128)(2,1)}, u32[]{:S(2)}, u32[]{:S(2)}) collective-permute-start(bf16[256,4096]{1,0:T(8,128)(2,1)} %bitcast.16), channel_id=1, source_target_pairs={{0,1},{1,0},{2,3},{3,2},{4,5},{5,4},{6,7},{7,6},{8,9},{9,8},{10,11... | collective-permute-start | bytes 6291464 | tf_op jit(solution)/shard_map/ppermute | solution.py:280
  7.6 5.6 %collective-permute-done.2.refs_1_ = bf16[1024,256]{1,0:T(8,128)(2,1)} collective-permute-done((bf16[1024,256]{1,0:T(8,128)(2,1)S(1)}, bf16[1024,256]{1,0:T(8,128)(2,1)}, u32[]{:S(2)}, u32[]{:S(2)}) %collective-permute-start.2) | collective-permute-done | bytes 524320 | tf_op jit(solution)/shard_map/ppermute | solution.py:277
  20.4 2.5 %shard_map.74 = (f32[512,4]{1,0:T(8,128)S(1)}, f32[4,512]{1,0:T(4,128)S(1)}, f32[4,512]{1,0:T(4,128)S(1)}, f32[2,512]{1,0:T(2,128)S(1)}, f32[512,128]{1,0:T(8,128)S(1)}) custom-call(s32[2]{0:T(128)S(1)} %pad_add_fusion.2.at_ref, f32[16,256]{1,0:T(8,128)S(1)} %collective-permute-done.4.mine_ref, f32[16,256]{1,0:T(8,128)S(1)} %collective-permute-done.5.other_ref), custom_call_target="tpu_custom_call" | custom-call | flops 16777216 | bytes 1048576 | tf_op jit(solution)/shard_map/pallas_call | solution.py:45
  25.6 2.5 %shard_map.73 = (f32[512,4]{1,0:T(8,128)S(1)}, f32[4,512]{1,0:T(4,128)S(1)}, f32[4,512]{1,0:T(4,128)S(1)}, f32[2,512]{1,0:T(2,128)S(1)}, f32[512,128]{1,0:T(8,128)S(1)}) custom-call(s32[2]{0:T(128)S(1)} %pad_add_fusion.2.at_ref, f32[16,256]{1,0:T(8,128)S(1)} %bitcast.24, f32[16,256]{1,0:T(8,128)S(1)} %collective-permute-done.1.other_ref), custom_call_target="tpu_custom_call" | custom-call | flops 16777216 | bytes 1048576 | tf_op jit(solution)/shard_map/pallas_call | solution.py:45
  33.1 5.6 %collective-permute-done.6.refs_3_ = bf16[1024,256]{1,0:T(8,128)(2,1)S(1)} collective-permute-done((bf16[1024,256]{1,0:T(8,128)(2,1)S(1)}, bf16[1024,256]{1,0:T(8,128)(2,1)S(1)}, u32[]{:S(2)}, u32[]{:S(2)}) %collective-permute-start.6) | collective-permute-done | bytes 524320 | tf_op jit(solution)/shard_map/ppermute | solution.py:277
  39.5 2.9 %collective-permute-start.9 = (bf16[1024,512]{1,0:T(8,128)(2,1)S(1)}, bf16[1024,512]{1,0:T(8,128)(2,1)S(1)}, u32[]{:S(2)}, u32[]{:S(2)}) collective-permute-start(bf16[1024,512]{1,0:T(8,128)(2,1)S(1)} %collective-permute-done.8.refs_1_), channel_id=1, source_target_pairs={{0,64},{1,193},{2,66},{3,195},{4,68},{5,197},{6,70},{7,199},{8,72}... | collective-permute-start | bytes 3145736 | tf_op jit(solution)/shard_map/ppermute | solution.py:277
  43.4 20.5 %collective-permute-done.11.mine_ref = bf16[256,4096]{1,0:T(8,128)(2,1)} collective-permute-done((bf16[256,4096]{1,0:T(8,128)(2,1)S(1)}, bf16[256,4096]{1,0:T(8,128)(2,1)}, u32[]{:S(2)}, u32[]{:S(2)}) %collective-permute-start.11) | collective-permute-done | bytes 2097184 | tf_op jit(solution)/shard_map/ppermute | solution.py:280
  70.3 3.2 %shard_map.75 = (bf16[512,128]{1,0:T(8,128)(2,1)S(1)}, f32[512,128]{1,0:T(8,128)S(1)}) custom-call(s32[5]{0:T(128)S(1)} %copy-done.34, bf16[256,4096]{1,0:T(8,128)(2,1)S(1)} %bitcast.18, bf16[256,4096]{1,0:T(8,128)(2,1)} %collective-permute-done.other_ref, f32[512,128]{1,0:T(8,128)S(1)} %get-tuple-element.43.gl_ref, bf16[1024,256]{1,0:T(8,128)(2,1)S(1)} %fusion.1.refs_0_, ...), custom_call_target="tpu_custom_call" | custom-call | flops 1073741824 | bytes 8388608 | tf_op jit(solution)/shard_map/pallas_call | solution.py:45
  75.7 3.6 %shard_map.76.refs_0_ = f32[512,512]{1,0:T(8,128)S(1)} custom-call(s32[4]{0:T(128)S(1)} %pad_add_fusion.3.off_ref, bf16[256,4096]{1,0:T(8,128)(2,1)S(1)} %bitcast.19, bf16[256,4096]{1,0:T(8,128)(2,1)} %collective-permute-done.other_ref, bf16[1024,512]{1,0:T(8,128)(2,1)S(1)} %copy-done.3, bf16[1024,512]{1,0:T(8,128)(2,1)S(1)} %copy-done.7, ...), custom_call_target="tpu_custom_call" | custom-call | flops 1610612736 | bytes 8388608 | tf_op jit(solution)/shard_map/pallas_call | solution.py:45
  79.4 3.7 %shard_map.78 = (bf16[512,128]{1,0:T(8,128)(2,1)S(1)}, f32[512,128]{1,0:T(8,128)S(1)}) custom-call(s32[5]{0:T(128)S(1)} %copy-done.35, bf16[256,4096]{1,0:T(8,128)(2,1)} %collective-permute-done.11.mine_ref, bf16[256,4096]{1,0:T(8,128)(2,1)} %collective-permute-done.12.other_ref, f32[512,128]{1,0:T(8,128)S(1)} %copy-done.29, ...), custom_call_target="tpu_custom_call" | custom-call | flops 1073741824 | bytes 8388608 | tf_op jit(solution)/shard_map/pallas_call | solution.py:45
  84.2 4.1 %shard_map.77.refs_0_ = f32[512,512]{1,0:T(8,128)S(1)} custom-call(s32[4]{0:T(128)S(1)} %pad_add_fusion.3.off_ref, bf16[256,4096]{1,0:T(8,128)(2,1)} %collective-permute-done.11.mine_ref, bf16[256,4096]{1,0:T(8,128)(2,1)} %collective-permute-done.12.other_ref, bf16[1024,512]{1,0:T(8,128)(2,1)S(1)} %copy-done.3, bf16[1024,512]{1,0:T(8,128)(2,1)S(1)} %copy-done.7, ...), custom_call_target="tpu_custom_call" | custom-call | flops 1610612736 | bytes 8388608 | tf_op jit(solution)/shard_map/pallas_call | solution.py:45
  89.0 2.4 %shard_map.79.v_ref = bf16[512,512]{1,0:T(8,128)(2,1)S(1)} custom-call(s32[2]{0:T(128)S(1)} %pad_add_fusion.4.off_ref, bf16[256,4096]{1,0:T(8,128)(2,1)S(1)} %bitcast.20, bf16[256,4096]{1,0:T(8,128)(2,1)} %collective-permute-done.other_ref, f32[512,512]{1,0:T(8,128)S(1)} %shard_map.76.refs_0_, bf16[1024,512]{1,0:T(8,128)(2,1)S(1)} %collective-permute-done.10.refs_1_), custom_call_target="tpu_custom_call" | custom-call | flops 536870912 | bytes 4194304 | tf_op jit(solution)/shard_map/pallas_call | solution.py:45
  92.5 3.0 %shard_map.81.v_ref = bf16[512,512]{1,0:T(8,128)(2,1)S(1)} custom-call(s32[2]{0:T(128)S(1)} %pad_add_fusion.4.off_ref, bf16[256,4096]{1,0:T(8,128)(2,1)} %collective-permute-done.11.mine_ref, bf16[256,4096]{1,0:T(8,128)(2,1)} %collective-permute-done.12.other_ref, f32[512,512]{1,0:T(8,128)S(1)} %shard_map.77.refs_0_, ...), custom_call_target="tpu_custom_call" | custom-call | flops 536870912 | bytes 4194304 | tf_op jit(solution)/shard_map/pallas_call | solution.py:45
  96.6 2.8 %collective-permute-start.14 = (bf16[144,512]{1,0:T(8,128)(2,1)S(1)}, bf16[144,512]{1,0:T(8,128)(2,1)S(1)}, u32[]{:S(2)}, u32[]{:S(2)}) collective-permute-start(bf16[144,512]{1,0:T(8,128)(2,1)S(1)} %shard_map.83.mine_ref), channel_id=1, source_target_pairs={{0,6},{1,7},{2,4},{3,5},{4,2},{5,3},{6,0},{7,1},{8,14},{9,15},{10,... | collective-permute-start | bytes 442376 | tf_op jit(solution)/shard_map/ppermute | solution.py:280
  99.5 3.9 %shard_map.84.base_ref = f32[512,512]{1,0:T(8,128)} custom-call(bf16[512,128]{1,0:T(8,128)(2,1)} %get-tuple-element.81.q_ref, bf16[512,128]{1,0:T(8,128)(2,1)} %copy-done.24, bf16[512,512]{1,0:T(8,128)(2,1)} %copy-done.5, f32[512,128]{1,0:T(8,128)} %copy-done.13, f32[512,4]{1,0:T(8,128)} %copy-done.26, f32[4,512]{1,0:T(4,128)} %copy-done.33, ...), custom_call_target="tpu_custom_call" | custom-call | flops 268435456 | bytes 8388608 | tf_op jit(solution)/shard_map/pallas_call | solution.py:45
  105.8 3.9 %shard_map.86.base_ref = f32[512,512]{1,0:T(8,128)} custom-call(bf16[512,128]{1,0:T(8,128)(2,1)} %get-tuple-element.84.q_ref, bf16[512,128]{1,0:T(8,128)(2,1)} %copy-done.23, bf16[512,512]{1,0:T(8,128)(2,1)} %copy-done.4, f32[512,128]{1,0:T(8,128)} %copy-done.12, f32[512,4]{1,0:T(8,128)} %copy-done.25, f32[4,512]{1,0:T(4,128)} %copy-done.32, ...), custom_call_target="tpu_custom_call" | custom-call | flops 268435456 | bytes 8388608 | tf_op jit(solution)/shard_map/pallas_call | solution.py:45
  109.8 2.8 %collective-permute-start.16 = (bf16[144,512]{1,0:T(8,128)(2,1)S(1)}, bf16[144,512]{1,0:T(8,128)(2,1)S(1)}, u32[]{:S(2)}, u32[]{:S(2)}) collective-permute-start(bf16[144,512]{1,0:T(8,128)(2,1)S(1)} %shard_map.87.mine_ref), channel_id=1, source_target_pairs={{0,24},{1,25},{2,26},{3,27},{4,28},{5,29},{6,30},{7,31},{8,16},{9,... | collective-permute-start | bytes 442376 | tf_op jit(solution)/shard_map/ppermute | solution.py:280
  115.8 5.0 %collective-permute-start.17 = (bf16[144,512]{1,0:T(8,128)(2,1)S(1)}, bf16[144,512]{1,0:T(8,128)(2,1)S(1)}, u32[]{:S(2)}, u32[]{:S(2)}) collective-permute-start(bf16[144,512]{1,0:T(8,128)(2,1)S(1)} %shard_map.88), channel_id=1, source_target_pairs={{0,56},{1,57},{2,58},{3,59},{4,60},{5,61},{6,62},{7,63},{8,48},{9,... | collective-permute-start | bytes 442376 | tf_op jit(solution)/shard_map/ppermute | solution.py:280
  121.5 3.4 %shard_map.90.base_ref = f32[512,512]{1,0:T(8,128)} custom-call(s32[2]{0:T(128)} %pad_add_fusion.at_ref, bf16[512,128]{1,0:T(8,128)(2,1)} %get-tuple-element.81.q_ref, f32[512,128]{1,0:T(8,128)} %copy-done.13, f32[1,512]{1,0:T(1,128)} %bitcast.25, f32[512,512]{1,0:T(8,128)} %shard_map.84.base_ref, bf16[144,512]{1,0:T(8,128)(2,1)} %copy-done.21, ...), custom_call_target="tpu_custom_call" | custom-call | flops 201326592 | bytes 4194304 | tf_op jit(solution)/shard_map/pallas_call | solution.py:45
  124.9 3.4 %shard_map.89.base_ref = f32[512,512]{1,0:T(8,128)} custom-call(s32[2]{0:T(128)} %pad_add_fusion.1.at_ref, bf16[512,128]{1,0:T(8,128)(2,1)} %get-tuple-element.84.q_ref, f32[512,128]{1,0:T(8,128)} %copy-done.12, f32[1,512]{1,0:T(1,128)} %bitcast.26, f32[512,512]{1,0:T(8,128)} %shard_map.86.base_ref, bf16[144,512]{1,0:T(8,128)(2,1)} %copy-done.20, ...), custom_call_target="tpu_custom_call" | custom-call | flops 201326592 | bytes 4194304 | tf_op jit(solution)/shard_map/pallas_call | solution.py:45
  129.0 3.7 %shard_map.92 = (bf16[256,512]{1,0:T(8,128)(2,1)}, bf16[256,512]{1,0:T(8,128)(2,1)}) custom-call(s32[3]{0:T(128)} %add_add_fusion.1.at_ref, bf16[512,128]{1,0:T(8,128)(2,1)} %get-tuple-element.81.q_ref, f32[512,128]{1,0:T(8,128)} %copy-done.13, f32[1,512]{1,0:T(1,128)} %bitcast.27, f32[512,512]{1,0:T(8,128)} %shard_map.90.base_ref, ...), custom_call_target="tpu_custom_call" | custom-call | flops 134217728 | bytes 4194304 | tf_op jit(solution)/shard_map/pallas_call | solution.py:45
  132.7 4.6 %collective-permute-start.20 = (bf16[256,512]{1,0:T(8,128)(2,1)}, bf16[256,512]{1,0:T(8,128)(2,1)S(1)}, u32[]{:S(2)}, u32[]{:S(2)}) collective-permute-start(bf16[256,512]{1,0:T(8,128)(2,1)} %get-tuple-element.80), channel_id=1, source_target_pairs={{0,3},{1,2},{2,1},{3,0},{4,7},{5,6},{6,5},{7,4},{8,11},{9,10},{10,... | collective-permute-start | bytes 786440 | tf_op jit(solution)/shard_map/ppermute | solution.py:280
  137.3 3.8 %shard_map.91 = (bf16[256,512]{1,0:T(8,128)(2,1)}, bf16[256,512]{1,0:T(8,128)(2,1)}) custom-call(s32[3]{0:T(128)} %add_add_fusion.at_ref, bf16[512,128]{1,0:T(8,128)(2,1)} %get-tuple-element.84.q_ref, f32[512,128]{1,0:T(8,128)} %copy-done.12, f32[1,512]{1,0:T(1,128)} %bitcast.28, f32[512,512]{1,0:T(8,128)} %shard_map.89.base_ref, ...), custom_call_target="tpu_custom_call" | custom-call | flops 134217728 | bytes 4194304 | tf_op jit(solution)/shard_map/pallas_call | solution.py:45
  141.1 5.7 %collective-permute-done.20.refs_3_ = bf16[256,512]{1,0:T(8,128)(2,1)S(1)} collective-permute-done((bf16[256,512]{1,0:T(8,128)(2,1)}, bf16[256,512]{1,0:T(8,128)(2,1)S(1)}, u32[]{:S(2)}, u32[]{:S(2)}) %collective-permute-start.20) | collective-permute-done | bytes 262176 | tf_op jit(solution)/shard_map/ppermute | solution.py:280
  (141 shorter events, 42.6 us)
Async XLA Ops:
  0.0 30.0 %collective-permute-start = (bf16[256,4096]{1,0:T(8,128)(2,1)}, bf16[256,4096]{1,0:T(8,128)(2,1)}, u32[]{:S(2)}, u32[]{:S(2)}) collective-permute-start(bf16[256,4096]{1,0:T(8,128)(2,1)} %bitcast.16), channel_id=1, source_target_pairs={{0,1},{1,0},{2,3},{3,2},{4,5},{5,4},{6,7},{7,6},{8,9},{9,8},{10,11... | collective-permute-start | bytes 6291464 | tf_op jit(solution)/shard_map/ppermute | solution.py:280
  4.7 8.5 %collective-permute-start.2 = (bf16[1024,256]{1,0:T(8,128)(2,1)S(1)}, bf16[1024,256]{1,0:T(8,128)(2,1)}, u32[]{:S(2)}, u32[]{:S(2)}) collective-permute-start(bf16[1024,256]{1,0:T(8,128)(2,1)S(1)} %fusion.1.refs_0_), channel_id=1, source_target_pairs={{0,64},{1,193},{2,66},{3,195},{4,68},{5,197},{6,70},{7,199},{8,72}... | collective-permute-start | bytes 1572872 | tf_op jit(solution)/shard_map/ppermute | solution.py:277
  5.9 11.7 %collective-permute-start.4 = (f32[16,256]{1,0:T(8,128)S(1)}, f32[16,256]{1,0:T(8,128)S(1)}, u32[]{:S(2)}, u32[]{:S(2)}) collective-permute-start(f32[16,256]{1,0:T(8,128)S(1)} %bitcast.21), channel_id=1, source_target_pairs={{0,2},{1,3},{2,0},{3,1},{4,6},{5,7},{6,4},{7,5},{8,10},{9,11},{10,... | collective-permute-start | bytes 49160 | tf_op jit(solution)/shard_map/ppermute | solution.py:280
  7.2 10.4 %collective-permute-start.5 = (f32[16,256]{1,0:T(8,128)S(1)}, f32[16,256]{1,0:T(8,128)S(1)}, u32[]{:S(2)}, u32[]{:S(2)}) collective-permute-start(f32[16,256]{1,0:T(8,128)S(1)} %bitcast.22), channel_id=1, source_target_pairs={{0,3},{1,2},{2,1},{3,0},{4,7},{5,6},{6,5},{7,4},{8,11},{9,10},{10,... | collective-permute-start | bytes 49160 | tf_op jit(solution)/shard_map/ppermute | solution.py:280
  13.2 16.8 %collective-permute-start.3 = (bf16[1024,256]{1,0:T(8,128)(2,1)}, bf16[1024,256]{1,0:T(8,128)(2,1)S(1)}, u32[]{:S(2)}, u32[]{:S(2)}) collective-permute-start(bf16[1024,256]{1,0:T(8,128)(2,1)} %collective-permute-done.2.refs_1_), channel_id=1, source_target_pairs={{0,64},{1,193},{2,66},{3,195},{4,68},{5,197},{6,70},{7,199},{8,72}... | collective-permute-start | bytes 1572872 | tf_op jit(solution)/shard_map/ppermute | solution.py:277
  16.5 16.5 %collective-permute-start.8 = (bf16[1024,512]{1,0:T(8,128)(2,1)S(1)}, bf16[1024,512]{1,0:T(8,128)(2,1)S(1)}, u32[]{:S(2)}, u32[]{:S(2)}) collective-permute-start(bf16[1024,512]{1,0:T(8,128)(2,1)S(1)} %constant_dynamic-slice_fusion.refs_0_), channel_id=1, source_target_pairs={{0,64},{1,193},{2,66},{3,195},{4,68},{5,197},{6,70},{7,199},{8,72}... | collective-permute-start | bytes 3145736 | tf_op jit(solution)/shard_map/ppermute | solution.py:277
  17.6 46.2 %collective-permute-start.11 = (bf16[256,4096]{1,0:T(8,128)(2,1)S(1)}, bf16[256,4096]{1,0:T(8,128)(2,1)}, u32[]{:S(2)}, u32[]{:S(2)}) collective-permute-start(bf16[256,4096]{1,0:T(8,128)(2,1)S(1)} %bitcast.17), channel_id=1, source_target_pairs={{0,2},{1,3},{2,0},{3,1},{4,6},{5,7},{6,4},{7,5},{8,10},{9,11},{10,... | collective-permute-start | bytes 6291464 | tf_op jit(solution)/shard_map/ppermute | solution.py:280
  19.0 5.9 %collective-permute-start.1 = (f32[16,256]{1,0:T(8,128)S(1)}, f32[16,256]{1,0:T(8,128)S(1)}, u32[]{:S(2)}, u32[]{:S(2)}) collective-permute-start(f32[16,256]{1,0:T(8,128)S(1)} %bitcast.23), channel_id=1, source_target_pairs={{0,1},{1,0},{2,3},{3,2},{4,5},{5,4},{6,7},{7,6},{8,9},{9,8},{10,11... | collective-permute-start | bytes 49160 | tf_op jit(solution)/shard_map/ppermute | solution.py:280
  24.9 38.9 %copy-start.36 = (f32[2,512]{1,0:T(2,128)}, f32[2,512]{1,0:T(2,128)S(1)}, u32[]{:S(2)}) copy-start(f32[2,512]{1,0:T(2,128)S(1)} %get-tuple-element.61.logs_ref) | copy-start | bytes 12292
  30.0 8.7 %collective-permute-start.6 = (bf16[1024,256]{1,0:T(8,128)(2,1)S(1)}, bf16[1024,256]{1,0:T(8,128)(2,1)S(1)}, u32[]{:S(2)}, u32[]{:S(2)}) collective-permute-start(bf16[1024,256]{1,0:T(8,128)(2,1)S(1)} %collective-permute-done.3.refs_2_), channel_id=1, source_target_pairs={{0,64},{1,193},{2,66},{3,195},{4,68},{5,197},{6,70},{7,199},{8,72}... | collective-permute-start | bytes 1572872 | tf_op jit(solution)/shard_map/ppermute | solution.py:277
  39.5 24.3 %collective-permute-start.9 = (bf16[1024,512]{1,0:T(8,128)(2,1)S(1)}, bf16[1024,512]{1,0:T(8,128)(2,1)S(1)}, u32[]{:S(2)}, u32[]{:S(2)}) collective-permute-start(bf16[1024,512]{1,0:T(8,128)(2,1)S(1)} %collective-permute-done.8.refs_1_), channel_id=1, source_target_pairs={{0,64},{1,193},{2,66},{3,195},{4,68},{5,197},{6,70},{7,199},{8,72}... | collective-permute-start | bytes 3145736 | tf_op jit(solution)/shard_map/ppermute | solution.py:277
  64.9 14.4 %collective-permute-start.12 = (bf16[256,4096]{1,0:T(8,128)(2,1)}, bf16[256,4096]{1,0:T(8,128)(2,1)}, u32[]{:S(2)}, u32[]{:S(2)}) collective-permute-start(bf16[256,4096]{1,0:T(8,128)(2,1)} %collective-permute-done.11.mine_ref), channel_id=1, source_target_pairs={{0,1},{1,0},{2,3},{3,2},{4,5},{5,4},{6,7},{7,6},{8,9},{9,8},{10,11... | collective-permute-start | bytes 6291464 | tf_op jit(solution)/shard_map/ppermute | solution.py:280
  73.5 1.4 collective-permute-start.7
  73.6 15.4 %collective-permute-start.10 = (bf16[1024,512]{1,0:T(8,128)(2,1)S(1)}, bf16[1024,512]{1,0:T(8,128)(2,1)S(1)}, u32[]{:S(2)}, u32[]{:S(2)}) collective-permute-start(bf16[1024,512]{1,0:T(8,128)(2,1)S(1)} %copy-done.9), channel_id=1, source_target_pairs={{0,64},{1,193},{2,66},{3,195},{4,68},{5,197},{6,70},{7,199},{8,72}... | collective-permute-start | bytes 3145736 | tf_op jit(solution)/shard_map/ppermute | solution.py:277
  75.7 15.8 %copy-start.23 = (bf16[512,128]{1,0:T(8,128)(2,1)}, bf16[512,128]{1,0:T(8,128)(2,1)S(1)}, u32[]{:S(2)}) copy-start(bf16[512,128]{1,0:T(8,128)(2,1)S(1)} %get-tuple-element.52.k_ref) | copy-start | bytes 393220
  83.1 5.3 %collective-permute-start.13 = (bf16[512,128]{1,0:T(8,128)(2,1)S(1)}, bf16[512,128]{1,0:T(8,128)(2,1)S(1)}, u32[]{:S(2)}, u32[]{:S(2)}) collective-permute-start(bf16[512,128]{1,0:T(8,128)(2,1)S(1)} %get-tuple-element.51), channel_id=1, source_target_pairs={{0,1},{1,0},{2,3},{3,2},{4,5},{5,4},{6,7},{7,6},{8,9},{9,8},{10,11... | collective-permute-start | bytes 393224 | tf_op jit(solution)/shard_map/ppermute | solution.py:280
  96.6 6.7 %collective-permute-start.14 = (bf16[144,512]{1,0:T(8,128)(2,1)S(1)}, bf16[144,512]{1,0:T(8,128)(2,1)S(1)}, u32[]{:S(2)}, u32[]{:S(2)}) collective-permute-start(bf16[144,512]{1,0:T(8,128)(2,1)S(1)} %shard_map.83.mine_ref), channel_id=1, source_target_pairs={{0,6},{1,7},{2,4},{3,5},{4,2},{5,3},{6,0},{7,1},{8,14},{9,15},{10,... | collective-permute-start | bytes 442376 | tf_op jit(solution)/shard_map/ppermute | solution.py:280
  103.4 18.1 %copy-start.10 = (bf16[144,512]{1,0:T(8,128)(2,1)}, bf16[144,512]{1,0:T(8,128)(2,1)S(1)}, u32[]{:S(2)}) copy-start(bf16[144,512]{1,0:T(8,128)(2,1)S(1)} %collective-permute-done.14.got_ref.refs_1_) | copy-start | bytes 442372
  103.4 6.3 %collective-permute-start.15 = (bf16[144,512]{1,0:T(8,128)(2,1)S(1)}, bf16[144,512]{1,0:T(8,128)(2,1)S(1)}, u32[]{:S(2)}, u32[]{:S(2)}) collective-permute-start(bf16[144,512]{1,0:T(8,128)(2,1)S(1)} %shard_map.85.mine_ref), channel_id=1, source_target_pairs={{0,8},{1,9},{2,10},{3,11},{4,12},{5,13},{6,14},{7,15},{8,0},{9,1},... | collective-permute-start | bytes 442376 | tf_op jit(solution)/shard_map/ppermute | solution.py:280
  109.8 6.0 %collective-permute-start.16 = (bf16[144,512]{1,0:T(8,128)(2,1)S(1)}, bf16[144,512]{1,0:T(8,128)(2,1)S(1)}, u32[]{:S(2)}, u32[]{:S(2)}) collective-permute-start(bf16[144,512]{1,0:T(8,128)(2,1)S(1)} %shard_map.87.mine_ref), channel_id=1, source_target_pairs={{0,24},{1,25},{2,26},{3,27},{4,28},{5,29},{6,30},{7,31},{8,16},{9,... | collective-permute-start | bytes 442376 | tf_op jit(solution)/shard_map/ppermute | solution.py:280
  115.8 12.5 %collective-permute-start.17 = (bf16[144,512]{1,0:T(8,128)(2,1)S(1)}, bf16[144,512]{1,0:T(8,128)(2,1)S(1)}, u32[]{:S(2)}, u32[]{:S(2)}) collective-permute-start(bf16[144,512]{1,0:T(8,128)(2,1)S(1)} %shard_map.88), channel_id=1, source_target_pairs={{0,56},{1,57},{2,58},{3,59},{4,60},{5,61},{6,62},{7,63},{8,48},{9,... | collective-permute-start | bytes 442376 | tf_op jit(solution)/shard_map/ppermute | solution.py:280
  132.7 8.4 %collective-permute-start.19 = (bf16[256,512]{1,0:T(8,128)(2,1)}, bf16[256,512]{1,0:T(8,128)(2,1)S(1)}, u32[]{:S(2)}, u32[]{:S(2)}) collective-permute-start(bf16[256,512]{1,0:T(8,128)(2,1)} %get-tuple-element.79), channel_id=1, source_target_pairs={{0,2},{1,3},{2,0},{3,1},{4,6},{5,7},{6,4},{7,5},{8,10},{9,11},{10,... | collective-permute-start | bytes 786440 | tf_op jit(solution)/shard_map/ppermute | solution.py:280
  132.7 14.1 %collective-permute-start.20 = (bf16[256,512]{1,0:T(8,128)(2,1)}, bf16[256,512]{1,0:T(8,128)(2,1)S(1)}, u32[]{:S(2)}, u32[]{:S(2)}) collective-permute-start(bf16[256,512]{1,0:T(8,128)(2,1)} %get-tuple-element.80), channel_id=1, source_target_pairs={{0,3},{1,2},{2,1},{3,0},{4,7},{5,6},{6,5},{7,4},{8,11},{9,10},{10,... | collective-permute-start | bytes 786440 | tf_op jit(solution)/shard_map/ppermute | solution.py:280
  141.1 5.7 %collective-permute-start.18 = (bf16[256,512]{1,0:T(8,128)(2,1)}, bf16[256,512]{1,0:T(8,128)(2,1)S(1)}, u32[]{:S(2)}, u32[]{:S(2)}) collective-permute-start(bf16[256,512]{1,0:T(8,128)(2,1)} %get-tuple-element.77), channel_id=1, source_target_pairs={{0,1},{1,0},{2,3},{3,2},{4,5},{5,4},{6,7},{7,6},{8,9},{9,8},{10,11... | collective-permute-start | bytes 786440 | tf_op jit(solution)/shard_map/ppermute | solution.py:280
  (40 other events, 139.7 us)

commit v3 on v2

--- a/solution.py
+++ b/solution.py
@@ -287,8 +287,6 @@
 
     mine = inputs[0]
     decay_mine = log_decay[0].T
-    decay_sib, decay_far, decay_farsib = [swap(decay_mine, m) for m in (1, 2, 3)]
-    far = swap(after(mine, decay_far, decay_farsib), 2)
     weights_v = [lax.dynamic_slice(value_weight, (0, quarter * wide), (rows, wide))]
     weights_s = [
         jnp.concatenate(
@@ -302,35 +300,66 @@
             axis=1,
         )
     ]
+    offsets = jnp.stack([(x - sign * i) % n_dp * rows for i in range(4)] + [core])
+    cut = BLOCK // 2
+    far_a = swap(mine[:cut], 2)
+    weights_v.append(px(weights_v[0]))
     weights_s.append(px(weights_s[0]))
-    weights_v.append(px(weights_v[0]))
+    decay_sib = swap(decay_mine, 1)
     sib = swap(mine, 1)
-    preps = []
-    for pair in ((decay_mine, decay_sib), (decay_far, decay_farsib)):
-        preps.append(
-            call(
-                prep_kernel,
-                (
-                    shape(2 * BLOCK, HPC, F32),
-                    shape(HPC, 2 * BLOCK, F32),
-                    shape(HPC, 2 * BLOCK, F32),
-                    shape(2, wide, F32),
-                    shape(2 * BLOCK, HALF, F32),
-                ),
-                (jnp.stack([core, quarter]), *pair),
-                smem=1,
-                flops=1 << 24,
-                nbytes=1 << 20,
-                mib=8,
-            )
-        )
+    weights_v[1], weights_s[1], far_a, sib, decay_sib, rest, decays = lax.optimization_barrier(
+        (weights_v[1], weights_s[1], far_a, sib, decay_sib, mine[cut:], decay_mine)
+    )
+    far_b = swap(rest, 2)
+    weights_v.append(px(weights_v[1]))
     weights_s.append(px(weights_s[1]))
-    weights_s.append(px(after(weights_s[2], preps[0][4], preps[1][4], sib)))
-    weights_v.append(px(after(weights_v[1], weights_s[3])))
+    decay_far = swap(jnp.concatenate([decays, decay_sib], axis=0), 2)
+    far_a_sib = swap(far_a, 1)
+
+    def prep(pair):
+        return call(
+            prep_kernel,
+            (
+                shape(2 * BLOCK, HPC, F32),
+                shape(HPC, 2 * BLOCK, F32),
+                shape(HPC, 2 * BLOCK, F32),
+                shape(2, wide, F32),
+                shape(2 * BLOCK, HALF, F32),
+            ),
+            (jnp.stack([core, quarter]), *pair),
+            smem=1,
+            flops=1 << 24,
+            nbytes=1 << 20,
+            mib=8,
+        )
+
+    preps = [prep((decays, decay_sib))]
+
+    def value(first, last, toks, base, kind):
+        return call(
+            functools.partial(value_kernel, last - first, base is None),
+            shape(2 * BLOCK, wide, kind),
+            (
+                jnp.concatenate([offsets[first:last], offsets[4:]]),
+                *toks,
+                *([] if base is None else [base]),
+                *weights_v[first:last],
+            ),
+            smem=1,
+            flops=2 * 512 * 1024 * (last - first) * wide,
+            nbytes=(4 + last - first) << 20,
+        )
+
+    parts = [value(0, 2, (mine, sib), None, F32)]
+    weights_v[2], weights_s[2], far_b, far_a_sib, decay_far, parts[0] = lax.optimization_barrier(
+        (weights_v[2], weights_s[2], far_b, far_a_sib, decay_far, parts[0])
+    )
+    far_b_sib = swap(far_b, 1)
     weights_v.append(px(weights_v[2]))
-    far = after(far, weights_v[2])
-    far_sib = swap(far, 1)
-    offsets = jnp.stack([(x - sign * i) % n_dp * rows for i in range(4)] + [core])
+    weights_s.append(px(weights_s[2]))
+    preps.append(prep((decay_far[:16], decay_far[16:])))
+    far = jnp.concatenate([far_a, far_b], axis=0)
+    far_sib = jnp.concatenate([far_a_sib, far_b_sib], axis=0)
 
     chips = []
     for late in range(2):
@@ -347,30 +376,18 @@
         fetched = swap(made, 1)
         q = jnp.where(core == 0, made, fetched)
         k = jnp.where(core == 0, fetched, made)
-        part = call(
-            functools.partial(value_kernel, 3, True),
-            shape(2 * BLOCK, wide, F32),
-            (jnp.concatenate([offsets[:3], offsets[4:]]), *toks, *weights_v[:3]),
-            smem=1,
-            flops=2 * 512 * 3072 * wide,
-            nbytes=8 << 20,
-        )
-        chips.append([q, k, lam, part])
-
-    last_v, *parts = lax.optimization_barrier((weights_v[3], chips[0][3], chips[1][3], chips[0][1], chips[1][1]))
+        if late:
+            parts.append(value(0, 3, toks, None, F32))
+        chips.append([q, k, lam])
+
+    weights_v[3], parts[1], chips[0][1], chips[1][1] = lax.optimization_barrier(
+        (weights_v[3], parts[1], chips[0][1], chips[1][1])
+    )
     for late in range(2):
         toks = (far, far_sib) if late else (mine, sib)
         cum, cum_t, remain, logs, gl = preps[late]
-        q, k, lam, _ = chips[late]
-        k = parts[2 + late]
-        v = call(
-            functools.partial(value_kernel, 1, False),
-            shape(2 * BLOCK, wide, BF16),
-            (offsets[3:], *toks, parts[late], last_v),
-            smem=1,
-            flops=2 * 512 * 1024 * wide,
-            nbytes=4 << 20,
-        )
+        q, k, lam = chips[late]
+        v = value(2 + late, 4, toks, parts[late], BF16)
         payload = shape(HALF + EXTRA, wide, BF16)
         low_state, send = call(
             state_kernel,

time: 149 us -> 145 us (0.973)
  waiting for transfers between devices: 39.7 us -> 46.6 us
  starting transfers between devices: 35.8 us -> 30.3 us
  local copies, waits for them, and re-layouts: 18.4 us -> 14.9 us
  Pallas kernels: 49.1 us -> 46.2 us
    unnamed x87 -> x49, local copies, waits for them, and re-layouts: 15.1 us -> 8.34 us
    ppermute x6, waiting for transfers between devices: 12 us -> 16.9 us  [px(): return lax.ppermute(a, ('dp', 'ctx'), ring_x(1, n_dp, n_ctx))]
    ppermute x6, starting transfers between devices: 7.97 us -> 4.99 us  [px(): return lax.ppermute(a, ('dp', 'ctx'), ring_x(1, n_dp, n_ctx))]
    pallas_call x21, Pallas kernels: 49.1 us -> 46.2 us  [call(): pl.pallas_call(kernel, out_shape=outs, in_specs=specs, out_specs=jax.tree...]
    ppermute x15 -> x16, starting transfers between devices: 27.9 us -> 25.3 us  [swap(): return lax.ppermute(a, 'ctx', xor_pairs(mask, n_ctx))]
    ppermute x15 -> x16, waiting for transfers between devices: 27.6 us -> 29.7 us  [swap(): return lax.ppermute(a, 'ctx', xor_pairs(mask, n_ctx))]
    slice x0 -> x2, local copies, waits for them, and re-layouts: none -> 1.54 us  [the longest x1 1.53 us: per_device(): mine[cut:]]
  transfers between devices with their start and end apart: 21 -> 22, of which waited for: 7 -> 8; matrix products, arithmetic and copies ran while one was open for 6% -> 10% of each run, Pallas kernels for 25% -> 25%
where the time goes in v3:
time: 145 us; the launch traced here: 144 us
  waiting for transfers between devices  46.6 us (32%)
  Pallas kernels  46.2 us (32%)
  starting transfers between devices  30.3 us (21%)
  local copies, waits for them, and re-layouts  14.9 us (10%)
  other arithmetic  5.29 us (4%)
    pallas_call x21, Pallas kernels, call(): pl.pallas_call(kernel, out_shape=outs, in_specs=specs, out_specs=jax.tree...  46.2 us
    ppermute x16, waiting for transfers between devices, swap(): return lax.ppermute(a, 'ctx', xor_pairs(mask, n_ctx))  29.7 us
    ppermute x16, starting transfers between devices, swap(): return lax.ppermute(a, 'ctx', xor_pairs(mask, n_ctx))  25.3 us
    ppermute x6, waiting for transfers between devices, px(): return lax.ppermute(a, ('dp', 'ctx'), ring_x(1, n_dp, n_ctx))  16.9 us
    unnamed x49, local copies, waits for them, and re-layouts  8.34 us
    ppermute x6, starting transfers between devices, px(): return lax.ppermute(a, ('dp', 'ctx'), ring_x(1, n_dp, n_ctx))  4.99 us
  transfers between devices with their start and end apart: 22, of which 8 were waited for; matrix products, arithmetic and copies ran while one was open for 10% of the time, Pallas kernels for 25%

profile of v3, /device:TPU:1, one launch (start us, length us, event | category | flops | bytes accessed | tf_op | source)
XLA Modules:
  0.0 143.6 jit_solution(15997472590040721422)
XLA Ops:
  0.0 3.2 %collective-permute-start.3 = (bf16[256,4096]{1,0:T(8,128)(2,1)}, bf16[256,4096]{1,0:T(8,128)(2,1)}, u32[]{:S(2)}, u32[]{:S(2)}) collective-permute-start(bf16[256,4096]{1,0:T(8,128)(2,1)} %bitcast.20), channel_id=1, source_target_pairs={{0,1},{1,0},{2,3},{3,2},{4,5},{5,4},{6,7},{7,6},{8,9},{9,8},{10,11... | collective-permute-start | bytes 6291464 | tf_op jit(solution)/shard_map/ppermute | solution.py:280
  3.2 2.3 %constant_dynamic-slice_fusion.1.refs_0_ = bf16[1024,512]{1,0:T(8,128)(2,1)} fusion(bf16[1024,2048]{1,0:T(8,128)(2,1)} %param.10, s32[]{:T(128)S(6)} %select_n.59), kind=kLoop, calls=%fused_computation.25 | loop fusion | bytes 2097156 | tf_op jit(solution)/shard_map/dynamic_slice | solution.py:290
  12.3 13.1 %collective-permute-done.1.refs_1_ = bf16[1024,256]{1,0:T(8,128)(2,1)} collective-permute-done((bf16[1024,256]{1,0:T(8,128)(2,1)S(1)}, bf16[1024,256]{1,0:T(8,128)(2,1)}, u32[]{:S(2)}, u32[]{:S(2)}) %collective-permute-start.1) | collective-permute-done | bytes 524320 | tf_op jit(solution)/shard_map/ppermute | solution.py:277
  25.4 7.6 %collective-permute-done.2 = bf16[128,4096]{1,0:T(8,128)(2,1)} collective-permute-done((bf16[128,4096]{1,0:T(8,128)(2,1)}, bf16[128,4096]{1,0:T(8,128)(2,1)}, u32[]{:S(2)}, u32[]{:S(2)}) %collective-permute-start.2) | collective-permute-done | bytes 1048608 | tf_op jit(solution)/shard_map/ppermute | solution.py:280
  39.5 3.4 %shard_map.74.refs_0_ = f32[512,512]{1,0:T(8,128)S(1)} custom-call(s32[3]{0:T(128)S(1)} %add_add_fusion.1.off_ref, bf16[256,4096]{1,0:T(8,128)(2,1)S(1)} %bitcast.21, bf16[256,4096]{1,0:T(8,128)(2,1)} %collective-permute-done.3.other_ref, bf16[1024,512]{1,0:T(8,128)(2,1)} %constant_dynamic-slice_fusion.1.refs_0_, bf16[1024,512]{1,0:T(8,128)(2,1)} %collective-permute-done.refs_1_), custom_call_target="tpu_custom_call" | custom-call | flops 1073741824 | bytes 6291456 | tf_op jit(solution)/shard_map/pallas_call | solution.py:45
  43.0 2.5 %shard_map.73 = (f32[512,4]{1,0:T(8,128)S(1)}, f32[4,512]{1,0:T(4,128)S(1)}, f32[4,512]{1,0:T(4,128)S(1)}, f32[2,512]{1,0:T(2,128)S(1)}, f32[512,128]{1,0:T(8,128)S(1)}) custom-call(s32[2]{0:T(128)S(1)} %pad_add_fusion.2.at_ref, f32[16,256]{1,0:T(8,128)S(1)} %bitcast.26, f32[16,256]{1,0:T(8,128)S(1)} %collective-permute-done.4.other_ref), custom_call_target="tpu_custom_call" | custom-call | flops 16777216 | bytes 1048576 | tf_op jit(solution)/shard_map/pallas_call | solution.py:45
  46.7 13.8 %collective-permute-done.9 = f32[32,256]{1,0:T(8,128)S(1)} collective-permute-done((f32[32,256]{1,0:T(8,128)S(1)}, f32[32,256]{1,0:T(8,128)S(1)}, u32[]{:S(2)}, u32[]{:S(2)}) %collective-permute-start.9) | collective-permute-done | bytes 32800 | tf_op jit(solution)/shard_map/ppermute | solution.py:280
  65.8 3.8 %collective-permute-done.10.refs_3_ = bf16[1024,256]{1,0:T(8,128)(2,1)S(1)} collective-permute-done((bf16[1024,256]{1,0:T(8,128)(2,1)S(1)}, bf16[1024,256]{1,0:T(8,128)(2,1)S(1)}, u32[]{:S(2)}, u32[]{:S(2)}) %collective-permute-start.10) | collective-permute-done | bytes 524320 | tf_op jit(solution)/shard_map/ppermute | solution.py:277
  69.6 3.0 %shard_map.75 = (bf16[512,128]{1,0:T(8,128)(2,1)S(1)}, f32[512,128]{1,0:T(8,128)S(1)}) custom-call(s32[5]{0:T(128)S(1)} %stack.63.off_ref, bf16[256,4096]{1,0:T(8,128)(2,1)S(1)} %bitcast.22, bf16[256,4096]{1,0:T(8,128)(2,1)} %collective-permute-done.3.other_ref, f32[512,128]{1,0:T(8,128)S(1)} %get-tuple-element.54.gl_ref, ...), custom_call_target="tpu_custom_call" | custom-call | flops 1073741824 | bytes 8388608 | tf_op jit(solution)/shard_map/pallas_call | solution.py:45
  72.7 2.2 %collective-permute-start.11 = (bf16[512,128]{1,0:T(8,128)(2,1)S(1)}, bf16[512,128]{1,0:T(8,128)(2,1)S(1)}, u32[]{:S(2)}, u32[]{:S(2)}) collective-permute-start(bf16[512,128]{1,0:T(8,128)(2,1)S(1)} %get-tuple-element.60), channel_id=1, source_target_pairs={{0,1},{1,0},{2,3},{3,2},{4,5},{5,4},{6,7},{7,6},{8,9},{9,8},{10,11... | collective-permute-start | bytes 393224 | tf_op jit(solution)/shard_map/ppermute | solution.py:280
  74.9 2.5 %shard_map.77 = (f32[512,4]{1,0:T(8,128)S(1)}, f32[4,512]{1,0:T(4,128)S(1)}, f32[4,512]{1,0:T(4,128)S(1)}, f32[2,512]{1,0:T(2,128)S(1)}, f32[512,128]{1,0:T(8,128)S(1)}) custom-call(s32[2]{0:T(128)S(1)} %pad_add_fusion.2.at_ref, f32[16,256]{1,0:T(8,128)S(1)} %get-tuple-element.104.mine_ref, f32[16,256]{1,0:T(8,128)S(1)} %get-tuple-element.103.other_ref), custom_call_target="tpu_custom_call" | custom-call | flops 16777216 | bytes 1048576 | tf_op jit(solution)/shard_map/pallas_call | solution.py:45
  79.5 2.4 %shard_map.78 = (bf16[512,128]{1,0:T(8,128)(2,1)S(1)}, f32[512,128]{1,0:T(8,128)S(1)}) custom-call(s32[5]{0:T(128)S(1)} %stack.63.off_ref, bf16[256,4096]{1,0:T(8,128)(2,1)S(1)} %constant_dynamic-update-slice_fusion.mine_ref, bf16[256,4096]{1,0:T(8,128)(2,1)S(1)} %constant_dynamic-update-slice_fusion.2.other_ref, f32[512,128]{1,0:T(8,128)S(1)} %get-tuple-element.66.gl_ref, ...), custom_call_target="tpu_custom_call" | custom-call | flops 1073741824 | bytes 8388608 | tf_op jit(solution)/shard_map/pallas_call | solution.py:45
  82.6 3.8 %shard_map.76.refs_0_ = f32[512,512]{1,0:T(8,128)S(1)} custom-call(s32[4]{0:T(128)S(1)} %pad_add_fusion.3.off_ref, bf16[256,4096]{1,0:T(8,128)(2,1)S(1)} %constant_dynamic-update-slice_fusion.mine_ref, bf16[256,4096]{1,0:T(8,128)(2,1)S(1)} %constant_dynamic-update-slice_fusion.2.other_ref, bf16[1024,512]{1,0:T(8,128)(2,1)} %constant_dynamic-slice_fusion.1.refs_0_, ...), custom_call_target="tpu_custom_call" | custom-call | flops 1610612736 | bytes 7340032 | tf_op jit(solution)/shard_map/pallas_call | solution.py:45
  87.1 3.2 %shard_map.79.v_ref = bf16[512,512]{1,0:T(8,128)(2,1)S(1)} custom-call(s32[3]{0:T(128)S(1)} %add_add_fusion.2.off_ref, bf16[256,4096]{1,0:T(8,128)(2,1)S(1)} %bitcast.23, bf16[256,4096]{1,0:T(8,128)(2,1)} %collective-permute-done.3.other_ref, f32[512,512]{1,0:T(8,128)S(1)} %shard_map.74.refs_0_, bf16[1024,512]{1,0:T(8,128)(2,1)} %collective-permute-done.5.refs_2_.refs_1_, ...), custom_call_target="tpu_custom_call" | custom-call | flops 1073741824 | bytes 6291456 | tf_op jit(solution)/shard_map/pallas_call | solution.py:45
  94.7 3.9 %shard_map.84.base_ref = f32[512,512]{1,0:T(8,128)} custom-call(bf16[512,128]{1,0:T(8,128)(2,1)} %get-tuple-element.99.q_ref, bf16[512,128]{1,0:T(8,128)(2,1)} %copy-done.12, bf16[512,512]{1,0:T(8,128)(2,1)} %copy-done.3, f32[512,128]{1,0:T(8,128)} %copy-done.7, f32[512,4]{1,0:T(8,128)} %copy-done.14, f32[4,512]{1,0:T(4,128)} %copy-done.20, ...), custom_call_target="tpu_custom_call" | custom-call | flops 268435456 | bytes 8388608 | tf_op jit(solution)/shard_map/pallas_call | solution.py:45
  101.0 3.9 %shard_map.86.base_ref = f32[512,512]{1,0:T(8,128)} custom-call(bf16[512,128]{1,0:T(8,128)(2,1)} %get-tuple-element.102.q_ref, bf16[512,128]{1,0:T(8,128)(2,1)} %copy-done.11, bf16[512,512]{1,0:T(8,128)(2,1)} %copy-done.2, f32[512,128]{1,0:T(8,128)} %copy-done.6, f32[512,4]{1,0:T(8,128)} %copy-done.13, f32[4,512]{1,0:T(4,128)} %copy-done.19, ...), custom_call_target="tpu_custom_call" | custom-call | flops 268435456 | bytes 8388608 | tf_op jit(solution)/shard_map/pallas_call | solution.py:45
  104.9 3.0 %collective-permute-start.17 = (bf16[144,512]{1,0:T(8,128)(2,1)S(1)}, bf16[144,512]{1,0:T(8,128)(2,1)S(1)}, u32[]{:S(2)}, u32[]{:S(2)}) collective-permute-start(bf16[144,512]{1,0:T(8,128)(2,1)S(1)} %shard_map.87.mine_ref), channel_id=1, source_target_pairs={{0,24},{1,25},{2,26},{3,27},{4,28},{5,29},{6,30},{7,31},{8,16},{9,... | collective-permute-start | bytes 442376 | tf_op jit(solution)/shard_map/ppermute | solution.py:280
  111.2 4.8 %collective-permute-start.18 = (bf16[144,512]{1,0:T(8,128)(2,1)S(1)}, bf16[144,512]{1,0:T(8,128)(2,1)S(1)}, u32[]{:S(2)}, u32[]{:S(2)}) collective-permute-start(bf16[144,512]{1,0:T(8,128)(2,1)S(1)} %shard_map.88), channel_id=1, source_target_pairs={{0,56},{1,57},{2,58},{3,59},{4,60},{5,61},{6,62},{7,63},{8,48},{9,... | collective-permute-start | bytes 442376 | tf_op jit(solution)/shard_map/ppermute | solution.py:280
  116.5 3.4 %shard_map.90.base_ref = f32[512,512]{1,0:T(8,128)} custom-call(s32[2]{0:T(128)} %pad_add_fusion.at_ref, bf16[512,128]{1,0:T(8,128)(2,1)} %get-tuple-element.99.q_ref, f32[512,128]{1,0:T(8,128)} %copy-done.7, f32[1,512]{1,0:T(1,128)} %bitcast.27, f32[512,512]{1,0:T(8,128)} %shard_map.84.base_ref, bf16[144,512]{1,0:T(8,128)(2,1)} %copy-done.9, ...), custom_call_target="tpu_custom_call" | custom-call | flops 201326592 | bytes 4194304 | tf_op jit(solution)/shard_map/pallas_call | solution.py:45
  119.9 3.4 %shard_map.89.base_ref = f32[512,512]{1,0:T(8,128)} custom-call(s32[2]{0:T(128)} %pad_add_fusion.1.at_ref, bf16[512,128]{1,0:T(8,128)(2,1)} %get-tuple-element.102.q_ref, f32[512,128]{1,0:T(8,128)} %copy-done.6, f32[1,512]{1,0:T(1,128)} %bitcast.28, f32[512,512]{1,0:T(8,128)} %shard_map.86.base_ref, bf16[144,512]{1,0:T(8,128)(2,1)} %copy-done.8, ...), custom_call_target="tpu_custom_call" | custom-call | flops 201326592 | bytes 4194304 | tf_op jit(solution)/shard_map/pallas_call | solution.py:45
  124.0 3.8 %shard_map.92 = (bf16[256,512]{1,0:T(8,128)(2,1)}, bf16[256,512]{1,0:T(8,128)(2,1)}) custom-call(s32[3]{0:T(128)} %add_add_fusion.3.at_ref, bf16[512,128]{1,0:T(8,128)(2,1)} %get-tuple-element.99.q_ref, f32[512,128]{1,0:T(8,128)} %copy-done.7, f32[1,512]{1,0:T(1,128)} %bitcast.29, f32[512,512]{1,0:T(8,128)} %shard_map.90.base_ref, ...), custom_call_target="tpu_custom_call" | custom-call | flops 134217728 | bytes 4194304 | tf_op jit(solution)/shard_map/pallas_call | solution.py:45
  127.8 4.2 %collective-permute-start.21 = (bf16[256,512]{1,0:T(8,128)(2,1)}, bf16[256,512]{1,0:T(8,128)(2,1)S(1)}, u32[]{:S(2)}, u32[]{:S(2)}) collective-permute-start(bf16[256,512]{1,0:T(8,128)(2,1)} %get-tuple-element.96), channel_id=1, source_target_pairs={{0,3},{1,2},{2,1},{3,0},{4,7},{5,6},{6,5},{7,4},{8,11},{9,10},{10,... | collective-permute-start | bytes 786440 | tf_op jit(solution)/shard_map/ppermute | solution.py:280
  132.0 3.8 %shard_map.91 = (bf16[256,512]{1,0:T(8,128)(2,1)}, bf16[256,512]{1,0:T(8,128)(2,1)}) custom-call(s32[3]{0:T(128)} %add_add_fusion.at_ref, bf16[512,128]{1,0:T(8,128)(2,1)} %get-tuple-element.102.q_ref, f32[512,128]{1,0:T(8,128)} %copy-done.6, f32[1,512]{1,0:T(1,128)} %bitcast.30, f32[512,512]{1,0:T(8,128)} %shard_map.89.base_ref, ...), custom_call_target="tpu_custom_call" | custom-call | flops 134217728 | bytes 4194304 | tf_op jit(solution)/shard_map/pallas_call | solution.py:45
  135.7 5.9 %collective-permute-done.21.refs_3_ = bf16[256,512]{1,0:T(8,128)(2,1)S(1)} collective-permute-done((bf16[256,512]{1,0:T(8,128)(2,1)}, bf16[256,512]{1,0:T(8,128)(2,1)S(1)}, u32[]{:S(2)}, u32[]{:S(2)}) %collective-permute-start.21) | collective-permute-done | bytes 262176 | tf_op jit(solution)/shard_map/ppermute | solution.py:280
  (112 shorter events, 36.5 us)
Async XLA Ops:
  0.0 33.0 %collective-permute-start.3 = (bf16[256,4096]{1,0:T(8,128)(2,1)}, bf16[256,4096]{1,0:T(8,128)(2,1)}, u32[]{:S(2)}, u32[]{:S(2)}) collective-permute-start(bf16[256,4096]{1,0:T(8,128)(2,1)} %bitcast.20), channel_id=1, source_target_pairs={{0,1},{1,0},{2,3},{3,2},{4,5},{5,4},{6,7},{7,6},{8,9},{9,8},{10,11... | collective-permute-start | bytes 6291464 | tf_op jit(solution)/shard_map/ppermute | solution.py:280
  5.5 19.9 %collective-permute-start = (bf16[1024,512]{1,0:T(8,128)(2,1)}, bf16[1024,512]{1,0:T(8,128)(2,1)}, u32[]{:S(2)}, u32[]{:S(2)}) collective-permute-start(bf16[1024,512]{1,0:T(8,128)(2,1)} %constant_dynamic-slice_fusion.1.refs_0_), channel_id=1, source_target_pairs={{0,64},{1,193},{2,66},{3,195},{4,68},{5,197},{6,70},{7,199},{8,72}... | collective-permute-start | bytes 3145736 | tf_op jit(solution)/shard_map/ppermute | solution.py:277
  7.8 25.1 %collective-permute-start.2 = (bf16[128,4096]{1,0:T(8,128)(2,1)}, bf16[128,4096]{1,0:T(8,128)(2,1)}, u32[]{:S(2)}, u32[]{:S(2)}) collective-permute-start(bf16[128,4096]{1,0:T(8,128)(2,1)} %get-tuple-element.98), channel_id=1, source_target_pairs={{0,2},{1,3},{2,0},{3,1},{4,6},{5,7},{6,4},{7,5},{8,10},{9,11},{10,... | collective-permute-start | bytes 3145736 | tf_op jit(solution)/shard_map/ppermute | solution.py:280
  10.4 14.9 %collective-permute-start.1 = (bf16[1024,256]{1,0:T(8,128)(2,1)S(1)}, bf16[1024,256]{1,0:T(8,128)(2,1)}, u32[]{:S(2)}, u32[]{:S(2)}) collective-permute-start(bf16[1024,256]{1,0:T(8,128)(2,1)S(1)} %fusion.1.refs_0_), channel_id=1, source_target_pairs={{0,64},{1,193},{2,66},{3,195},{4,68},{5,197},{6,70},{7,199},{8,72}... | collective-permute-start | bytes 1572872 | tf_op jit(solution)/shard_map/ppermute | solution.py:277
  11.1 1.2 collective-permute-start.4
  33.0 27.5 %collective-permute-start.5 = (bf16[1024,512]{1,0:T(8,128)(2,1)}, bf16[1024,512]{1,0:T(8,128)(2,1)}, u32[]{:S(2)}, u32[]{:S(2)}) collective-permute-start(bf16[1024,512]{1,0:T(8,128)(2,1)} %collective-permute-done.refs_1_), channel_id=1, source_target_pairs={{0,64},{1,193},{2,66},{3,195},{4,68},{5,197},{6,70},{7,199},{8,72}... | collective-permute-start | bytes 3145736 | tf_op jit(solution)/shard_map/ppermute | solution.py:277
  33.0 27.5 %collective-permute-start.8 = (bf16[128,4096]{1,0:T(8,128)(2,1)}, bf16[128,4096]{1,0:T(8,128)(2,1)}, u32[]{:S(2)}, u32[]{:S(2)}) collective-permute-start(bf16[128,4096]{1,0:T(8,128)(2,1)} %collective-permute-done.2), channel_id=1, source_target_pairs={{0,1},{1,0},{2,3},{3,2},{4,5},{5,4},{6,7},{7,6},{8,9},{9,8},{10,11... | collective-permute-start | bytes 3145736 | tf_op jit(solution)/shard_map/ppermute | solution.py:280
  34.7 25.8 %collective-permute-start.7 = (bf16[128,4096]{1,0:T(8,128)(2,1)}, bf16[128,4096]{1,0:T(8,128)(2,1)}, u32[]{:S(2)}, u32[]{:S(2)}) collective-permute-start(bf16[128,4096]{1,0:T(8,128)(2,1)} %get-tuple-element.57), channel_id=1, source_target_pairs={{0,2},{1,3},{2,0},{3,1},{4,6},{5,7},{6,4},{7,5},{8,10},{9,11},{10,... | collective-permute-start | bytes 3145736 | tf_op jit(solution)/shard_map/ppermute | solution.py:280
  35.1 25.4 %collective-permute-start.9 = (f32[32,256]{1,0:T(8,128)S(1)}, f32[32,256]{1,0:T(8,128)S(1)}, u32[]{:S(2)}, u32[]{:S(2)}) collective-permute-start(f32[32,256]{1,0:T(8,128)S(1)} %pad_maximum_fusion), channel_id=1, source_target_pairs={{0,2},{1,3},{2,0},{3,1},{4,6},{5,7},{6,4},{7,5},{8,10},{9,11},{10,... | collective-permute-start | bytes 98312 | tf_op jit(solution)/shard_map/ppermute | solution.py:280
  36.6 23.9 %collective-permute-start.6 = (bf16[1024,256]{1,0:T(8,128)(2,1)}, bf16[1024,256]{1,0:T(8,128)(2,1)S(1)}, u32[]{:S(2)}, u32[]{:S(2)}) collective-permute-start(bf16[1024,256]{1,0:T(8,128)(2,1)} %collective-permute-done.1.refs_1_), channel_id=1, source_target_pairs={{0,64},{1,193},{2,66},{3,195},{4,68},{5,197},{6,70},{7,199},{8,72}... | collective-permute-start | bytes 1572872 | tf_op jit(solution)/shard_map/ppermute | solution.py:277
  60.5 18.9 %collective-permute-start.13 = (bf16[128,4096]{1,0:T(8,128)(2,1)}, bf16[128,4096]{1,0:T(8,128)(2,1)S(1)}, u32[]{:S(2)}, u32[]{:S(2)}) collective-permute-start(bf16[128,4096]{1,0:T(8,128)(2,1)} %collective-permute-done.7), channel_id=1, source_target_pairs={{0,1},{1,0},{2,3},{3,2},{4,5},{5,4},{6,7},{7,6},{8,9},{9,8},{10,11... | collective-permute-start | bytes 3145736 | tf_op jit(solution)/shard_map/ppermute | solution.py:280
  61.3 8.3 %collective-permute-start.10 = (bf16[1024,256]{1,0:T(8,128)(2,1)S(1)}, bf16[1024,256]{1,0:T(8,128)(2,1)S(1)}, u32[]{:S(2)}, u32[]{:S(2)}) collective-permute-start(bf16[1024,256]{1,0:T(8,128)(2,1)S(1)} %collective-permute-done.6.refs_2_), channel_id=1, source_target_pairs={{0,64},{1,193},{2,66},{3,195},{4,68},{5,197},{6,70},{7,199},{8,72}... | collective-permute-start | bytes 1572872 | tf_op jit(solution)/shard_map/ppermute | solution.py:277
  64.2 22.9 %collective-permute-start.12 = (bf16[1024,512]{1,0:T(8,128)(2,1)}, bf16[1024,512]{1,0:T(8,128)(2,1)S(1)}, u32[]{:S(2)}, u32[]{:S(2)}) collective-permute-start(bf16[1024,512]{1,0:T(8,128)(2,1)} %collective-permute-done.5.refs_2_.refs_1_), channel_id=1, source_target_pairs={{0,64},{1,193},{2,66},{3,195},{4,68},{5,197},{6,70},{7,199},{8,72}... | collective-permute-start | bytes 3145736 | tf_op jit(solution)/shard_map/ppermute | solution.py:277
  72.7 6.0 %collective-permute-start.11 = (bf16[512,128]{1,0:T(8,128)(2,1)S(1)}, bf16[512,128]{1,0:T(8,128)(2,1)S(1)}, u32[]{:S(2)}, u32[]{:S(2)}) collective-permute-start(bf16[512,128]{1,0:T(8,128)(2,1)S(1)} %get-tuple-element.60), channel_id=1, source_target_pairs={{0,1},{1,0},{2,3},{3,2},{4,5},{5,4},{6,7},{7,6},{8,9},{9,8},{10,11... | collective-permute-start | bytes 393224 | tf_op jit(solution)/shard_map/ppermute | solution.py:280
  82.6 3.8 %collective-permute-start.14 = (bf16[512,128]{1,0:T(8,128)(2,1)S(1)}, bf16[512,128]{1,0:T(8,128)(2,1)S(1)}, u32[]{:S(2)}, u32[]{:S(2)}) collective-permute-start(bf16[512,128]{1,0:T(8,128)(2,1)S(1)} %get-tuple-element.67), channel_id=1, source_target_pairs={{0,1},{1,0},{2,3},{3,2},{4,5},{5,4},{6,7},{7,6},{8,9},{9,8},{10,11... | collective-permute-start | bytes 393224 | tf_op jit(solution)/shard_map/ppermute | solution.py:280
  92.0 12.8 %copy-start.9 = (bf16[144,512]{1,0:T(8,128)(2,1)}, bf16[144,512]{1,0:T(8,128)(2,1)S(1)}, u32[]{:S(2)}) copy-start(bf16[144,512]{1,0:T(8,128)(2,1)S(1)} %get-tuple-element.73.mine_ref.refs_0_) | copy-start | bytes 442372
  93.1 6.2 %collective-permute-start.15 = (bf16[144,512]{1,0:T(8,128)(2,1)S(1)}, bf16[144,512]{1,0:T(8,128)(2,1)S(1)}, u32[]{:S(2)}, u32[]{:S(2)}) collective-permute-start(bf16[144,512]{1,0:T(8,128)(2,1)S(1)} %shard_map.83.mine_ref), channel_id=1, source_target_pairs={{0,6},{1,7},{2,4},{3,5},{4,2},{5,3},{6,0},{7,1},{8,14},{9,15},{10,... | collective-permute-start | bytes 442376 | tf_op jit(solution)/shard_map/ppermute | solution.py:280
  99.3 17.2 %copy-start.4 = (bf16[144,512]{1,0:T(8,128)(2,1)}, bf16[144,512]{1,0:T(8,128)(2,1)S(1)}, u32[]{:S(2)}) copy-start(bf16[144,512]{1,0:T(8,128)(2,1)S(1)} %collective-permute-done.15.got_ref.refs_1_) | copy-start | bytes 442372
  99.4 5.4 %collective-permute-start.16 = (bf16[144,512]{1,0:T(8,128)(2,1)S(1)}, bf16[144,512]{1,0:T(8,128)(2,1)S(1)}, u32[]{:S(2)}, u32[]{:S(2)}) collective-permute-start(bf16[144,512]{1,0:T(8,128)(2,1)S(1)} %shard_map.85.mine_ref), channel_id=1, source_target_pairs={{0,8},{1,9},{2,10},{3,11},{4,12},{5,13},{6,14},{7,15},{8,0},{9,1},... | collective-permute-start | bytes 442376 | tf_op jit(solution)/shard_map/ppermute | solution.py:280
  104.9 6.2 %collective-permute-start.17 = (bf16[144,512]{1,0:T(8,128)(2,1)S(1)}, bf16[144,512]{1,0:T(8,128)(2,1)S(1)}, u32[]{:S(2)}, u32[]{:S(2)}) collective-permute-start(bf16[144,512]{1,0:T(8,128)(2,1)S(1)} %shard_map.87.mine_ref), channel_id=1, source_target_pairs={{0,24},{1,25},{2,26},{3,27},{4,28},{5,29},{6,30},{7,31},{8,16},{9,... | collective-permute-start | bytes 442376 | tf_op jit(solution)/shard_map/ppermute | solution.py:280
  111.2 12.1 %collective-permute-start.18 = (bf16[144,512]{1,0:T(8,128)(2,1)S(1)}, bf16[144,512]{1,0:T(8,128)(2,1)S(1)}, u32[]{:S(2)}, u32[]{:S(2)}) collective-permute-start(bf16[144,512]{1,0:T(8,128)(2,1)S(1)} %shard_map.88), channel_id=1, source_target_pairs={{0,56},{1,57},{2,58},{3,59},{4,60},{5,61},{6,62},{7,63},{8,48},{9,... | collective-permute-start | bytes 442376 | tf_op jit(solution)/shard_map/ppermute | solution.py:280
  127.8 8.0 %collective-permute-start.20 = (bf16[256,512]{1,0:T(8,128)(2,1)}, bf16[256,512]{1,0:T(8,128)(2,1)S(1)}, u32[]{:S(2)}, u32[]{:S(2)}) collective-permute-start(bf16[256,512]{1,0:T(8,128)(2,1)} %get-tuple-element.95), channel_id=1, source_target_pairs={{0,2},{1,3},{2,0},{3,1},{4,6},{5,7},{6,4},{7,5},{8,10},{9,11},{10,... | collective-permute-start | bytes 786440 | tf_op jit(solution)/shard_map/ppermute | solution.py:280
  127.8 13.9 %collective-permute-start.21 = (bf16[256,512]{1,0:T(8,128)(2,1)}, bf16[256,512]{1,0:T(8,128)(2,1)S(1)}, u32[]{:S(2)}, u32[]{:S(2)}) collective-permute-start(bf16[256,512]{1,0:T(8,128)(2,1)} %get-tuple-element.96), channel_id=1, source_target_pairs={{0,3},{1,2},{2,1},{3,0},{4,7},{5,6},{6,5},{7,4},{8,11},{9,10},{10,... | collective-permute-start | bytes 786440 | tf_op jit(solution)/shard_map/ppermute | solution.py:280
  135.7 5.9 %collective-permute-start.19 = (bf16[256,512]{1,0:T(8,128)(2,1)}, bf16[256,512]{1,0:T(8,128)(2,1)S(1)}, u32[]{:S(2)}, u32[]{:S(2)}) collective-permute-start(bf16[256,512]{1,0:T(8,128)(2,1)} %get-tuple-element.93), channel_id=1, source_target_pairs={{0,1},{1,0},{2,3},{3,2},{4,5},{5,4},{6,7},{7,6},{8,9},{9,8},{10,11... | collective-permute-start | bytes 786440 | tf_op jit(solution)/shard_map/ppermute | solution.py:280
  (21 other events, 95.6 us)

commit v4 on v3

--- a/solution.py
+++ b/solution.py
@@ -19,7 +19,7 @@
 HPC = 4
 MASKS = (6, 8, 24, 56)
 BIG = 56
-FINISH = BIG
+FINISH = 16
 EXTRA = 16
 
 

time: 145 us -> 141 us (0.972)
  Pallas kernels: 46.2 us -> 43 us
  waiting for transfers between devices: 46.6 us -> 48.6 us
  local copies, waits for them, and re-layouts: 14.9 us -> 13.4 us
    pallas_call x21, Pallas kernels: 46.2 us -> 43 us  [call(): pl.pallas_call(kernel, out_shape=outs, in_specs=specs, out_specs=jax.tree...]
    ppermute x16, waiting for transfers between devices: 29.7 us -> 31.6 us  [swap(): return lax.ppermute(a, 'ctx', xor_pairs(mask, n_ctx))]
    unnamed x49 -> x65, local copies, waits for them, and re-layouts: 8.34 us -> 6.8 us
where the time goes in v4:
time: 141 us; the launch traced here: 140 us
  waiting for transfers between devices  48.6 us (34%)
  Pallas kernels  43 us (30%)
  starting transfers between devices  30.5 us (22%)
  local copies, waits for them, and re-layouts  13.4 us (10%)
  other arithmetic  4.26 us (3%)
    pallas_call x21, Pallas kernels, call(): pl.pallas_call(kernel, out_shape=outs, in_specs=specs, out_specs=jax.tree...  43 us
    ppermute x16, waiting for transfers between devices, swap(): return lax.ppermute(a, 'ctx', xor_pairs(mask, n_ctx))  31.6 us
    ppermute x16, starting transfers between devices, swap(): return lax.ppermute(a, 'ctx', xor_pairs(mask, n_ctx))  25.5 us
    ppermute x6, waiting for transfers between devices, px(): return lax.ppermute(a, ('dp', 'ctx'), ring_x(1, n_dp, n_ctx))  16.9 us
    unnamed x65, local copies, waits for them, and re-layouts  6.8 us
    ppermute x6, starting transfers between devices, px(): return lax.ppermute(a, ('dp', 'ctx'), ring_x(1, n_dp, n_ctx))  4.99 us
  transfers between devices with their start and end apart: 22, of which 8 were waited for; matrix products, arithmetic and copies ran while one was open for 10% of the time, Pallas kernels for 25%

profile of v4, /device:TPU:1, one launch (start us, length us, event | category | flops | bytes accessed | tf_op | source)
XLA Modules:
  0.0 140.2 jit_solution(1462974808086210933)
XLA Ops:
  0.0 3.2 %collective-permute-start.3 = (bf16[256,4096]{1,0:T(8,128)(2,1)}, bf16[256,4096]{1,0:T(8,128)(2,1)}, u32[]{:S(2)}, u32[]{:S(2)}) collective-permute-start(bf16[256,4096]{1,0:T(8,128)(2,1)} %bitcast.20), channel_id=1, source_target_pairs={{0,1},{1,0},{2,3},{3,2},{4,5},{5,4},{6,7},{7,6},{8,9},{9,8},{10,11... | collective-permute-start | bytes 6291464 | tf_op jit(solution)/shard_map/ppermute | solution.py:280
  3.2 2.3 %constant_dynamic-slice_fusion.1.refs_0_ = bf16[1024,512]{1,0:T(8,128)(2,1)} fusion(bf16[1024,2048]{1,0:T(8,128)(2,1)} %param.10, s32[]{:T(128)S(6)} %select_n.59), kind=kLoop, calls=%fused_computation.25 | loop fusion | bytes 2097156 | tf_op jit(solution)/shard_map/dynamic_slice | solution.py:290
  12.3 13.1 %collective-permute-done.1.refs_1_ = bf16[1024,256]{1,0:T(8,128)(2,1)} collective-permute-done((bf16[1024,256]{1,0:T(8,128)(2,1)S(1)}, bf16[1024,256]{1,0:T(8,128)(2,1)}, u32[]{:S(2)}, u32[]{:S(2)}) %collective-permute-start.1) | collective-permute-done | bytes 524320 | tf_op jit(solution)/shard_map/ppermute | solution.py:277
  25.4 7.6 %collective-permute-done.2 = bf16[128,4096]{1,0:T(8,128)(2,1)} collective-permute-done((bf16[128,4096]{1,0:T(8,128)(2,1)}, bf16[128,4096]{1,0:T(8,128)(2,1)}, u32[]{:S(2)}, u32[]{:S(2)}) %collective-permute-start.2) | collective-permute-done | bytes 1048608 | tf_op jit(solution)/shard_map/ppermute | solution.py:280
  39.5 3.4 %shard_map.74.refs_0_ = f32[512,512]{1,0:T(8,128)S(1)} custom-call(s32[3]{0:T(128)S(1)} %add_add_fusion.1.off_ref, bf16[256,4096]{1,0:T(8,128)(2,1)S(1)} %bitcast.21, bf16[256,4096]{1,0:T(8,128)(2,1)} %collective-permute-done.3.other_ref, bf16[1024,512]{1,0:T(8,128)(2,1)} %constant_dynamic-slice_fusion.1.refs_0_, bf16[1024,512]{1,0:T(8,128)(2,1)} %collective-permute-done.refs_1_), custom_call_target="tpu_custom_call" | custom-call | flops 1073741824 | bytes 6291456 | tf_op jit(solution)/shard_map/pallas_call | solution.py:45
  43.0 2.5 %shard_map.73 = (f32[512,4]{1,0:T(8,128)S(1)}, f32[4,512]{1,0:T(4,128)S(1)}, f32[4,512]{1,0:T(4,128)S(1)}, f32[2,512]{1,0:T(2,128)S(1)}, f32[512,128]{1,0:T(8,128)S(1)}) custom-call(s32[2]{0:T(128)S(1)} %pad_add_fusion.2.at_ref, f32[16,256]{1,0:T(8,128)S(1)} %bitcast.30, f32[16,256]{1,0:T(8,128)S(1)} %collective-permute-done.4.other_ref), custom_call_target="tpu_custom_call" | custom-call | flops 16777216 | bytes 1048576 | tf_op jit(solution)/shard_map/pallas_call | solution.py:45
  46.8 13.8 %collective-permute-done.9 = f32[32,256]{1,0:T(8,128)S(1)} collective-permute-done((f32[32,256]{1,0:T(8,128)S(1)}, f32[32,256]{1,0:T(8,128)S(1)}, u32[]{:S(2)}, u32[]{:S(2)}) %collective-permute-start.9) | collective-permute-done | bytes 32800 | tf_op jit(solution)/shard_map/ppermute | solution.py:280
  65.8 3.8 %collective-permute-done.10.refs_3_ = bf16[1024,256]{1,0:T(8,128)(2,1)S(1)} collective-permute-done((bf16[1024,256]{1,0:T(8,128)(2,1)S(1)}, bf16[1024,256]{1,0:T(8,128)(2,1)S(1)}, u32[]{:S(2)}, u32[]{:S(2)}) %collective-permute-start.10) | collective-permute-done | bytes 524320 | tf_op jit(solution)/shard_map/ppermute | solution.py:277
  69.6 3.0 %shard_map.75 = (bf16[512,128]{1,0:T(8,128)(2,1)S(1)}, f32[512,128]{1,0:T(8,128)S(1)}) custom-call(s32[5]{0:T(128)S(1)} %stack.63.off_ref, bf16[256,4096]{1,0:T(8,128)(2,1)S(1)} %bitcast.22, bf16[256,4096]{1,0:T(8,128)(2,1)} %collective-permute-done.3.other_ref, f32[512,128]{1,0:T(8,128)S(1)} %get-tuple-element.54.gl_ref, ...), custom_call_target="tpu_custom_call" | custom-call | flops 1073741824 | bytes 8388608 | tf_op jit(solution)/shard_map/pallas_call | solution.py:45
  72.7 2.2 %collective-permute-start.11 = (bf16[512,128]{1,0:T(8,128)(2,1)S(1)}, bf16[512,128]{1,0:T(8,128)(2,1)S(1)}, u32[]{:S(2)}, u32[]{:S(2)}) collective-permute-start(bf16[512,128]{1,0:T(8,128)(2,1)S(1)} %get-tuple-element.60), channel_id=1, source_target_pairs={{0,1},{1,0},{2,3},{3,2},{4,5},{5,4},{6,7},{7,6},{8,9},{9,8},{10,11... | collective-permute-start | bytes 393224 | tf_op jit(solution)/shard_map/ppermute | solution.py:280
  74.9 2.5 %shard_map.77 = (f32[512,4]{1,0:T(8,128)S(1)}, f32[4,512]{1,0:T(4,128)S(1)}, f32[4,512]{1,0:T(4,128)S(1)}, f32[2,512]{1,0:T(2,128)S(1)}, f32[512,128]{1,0:T(8,128)S(1)}) custom-call(s32[2]{0:T(128)S(1)} %pad_add_fusion.2.at_ref, f32[16,256]{1,0:T(8,128)S(1)} %get-tuple-element.104.mine_ref, f32[16,256]{1,0:T(8,128)S(1)} %get-tuple-element.103.other_ref), custom_call_target="tpu_custom_call" | custom-call | flops 16777216 | bytes 1048576 | tf_op jit(solution)/shard_map/pallas_call | solution.py:45
  79.5 2.4 %shard_map.78 = (bf16[512,128]{1,0:T(8,128)(2,1)S(1)}, f32[512,128]{1,0:T(8,128)S(1)}) custom-call(s32[5]{0:T(128)S(1)} %stack.63.off_ref, bf16[256,4096]{1,0:T(8,128)(2,1)S(1)} %constant_dynamic-update-slice_fusion.mine_ref, bf16[256,4096]{1,0:T(8,128)(2,1)S(1)} %constant_dynamic-update-slice_fusion.2.other_ref, f32[512,128]{1,0:T(8,128)S(1)} %get-tuple-element.66.gl_ref, ...), custom_call_target="tpu_custom_call" | custom-call | flops 1073741824 | bytes 8388608 | tf_op jit(solution)/shard_map/pallas_call | solution.py:45
  82.7 3.8 %shard_map.76.refs_0_ = f32[512,512]{1,0:T(8,128)S(1)} custom-call(s32[4]{0:T(128)S(1)} %pad_add_fusion.3.off_ref, bf16[256,4096]{1,0:T(8,128)(2,1)S(1)} %constant_dynamic-update-slice_fusion.mine_ref, bf16[256,4096]{1,0:T(8,128)(2,1)S(1)} %constant_dynamic-update-slice_fusion.2.other_ref, bf16[1024,512]{1,0:T(8,128)(2,1)} %constant_dynamic-slice_fusion.1.refs_0_, ...), custom_call_target="tpu_custom_call" | custom-call | flops 1610612736 | bytes 7340032 | tf_op jit(solution)/shard_map/pallas_call | solution.py:45
  87.2 3.2 %shard_map.79.v_ref = bf16[512,512]{1,0:T(8,128)(2,1)S(1)} custom-call(s32[3]{0:T(128)S(1)} %add_add_fusion.2.off_ref, bf16[256,4096]{1,0:T(8,128)(2,1)S(1)} %bitcast.23, bf16[256,4096]{1,0:T(8,128)(2,1)} %collective-permute-done.3.other_ref, f32[512,512]{1,0:T(8,128)S(1)} %shard_map.74.refs_0_, bf16[1024,512]{1,0:T(8,128)(2,1)} %collective-permute-done.5.refs_2_.refs_1_, ...), custom_call_target="tpu_custom_call" | custom-call | flops 1073741824 | bytes 6291456 | tf_op jit(solution)/shard_map/pallas_call | solution.py:45
  94.7 3.9 %shard_map.84.base_ref = f32[512,512]{1,0:T(8,128)} custom-call(bf16[512,128]{1,0:T(8,128)(2,1)} %get-tuple-element.99.q_ref, bf16[512,128]{1,0:T(8,128)(2,1)} %copy-done.21, bf16[512,512]{1,0:T(8,128)(2,1)} %copy-done.3, f32[512,128]{1,0:T(8,128)} %copy-done.12, f32[512,4]{1,0:T(8,128)} %copy-done.23, f32[4,512]{1,0:T(4,128)} %copy-done.29, ...), custom_call_target="tpu_custom_call" | custom-call | flops 268435456 | bytes 8388608 | tf_op jit(solution)/shard_map/pallas_call | solution.py:45
  101.1 3.9 %shard_map.86.base_ref = f32[512,512]{1,0:T(8,128)} custom-call(bf16[512,128]{1,0:T(8,128)(2,1)} %get-tuple-element.102.q_ref, bf16[512,128]{1,0:T(8,128)(2,1)} %copy-done.20, bf16[512,512]{1,0:T(8,128)(2,1)} %copy-done.2, f32[512,128]{1,0:T(8,128)} %copy-done.10, f32[512,4]{1,0:T(8,128)} %copy-done.22, f32[4,512]{1,0:T(4,128)} %copy-done.28, ...), custom_call_target="tpu_custom_call" | custom-call | flops 268435456 | bytes 8388608 | tf_op jit(solution)/shard_map/pallas_call | solution.py:45
  105.1 3.0 %collective-permute-start.17 = (bf16[144,512]{1,0:T(8,128)(2,1)S(1)}, bf16[144,512]{1,0:T(8,128)(2,1)S(1)}, u32[]{:S(2)}, u32[]{:S(2)}) collective-permute-start(bf16[144,512]{1,0:T(8,128)(2,1)S(1)} %shard_map.87.mine_ref), channel_id=1, source_target_pairs={{0,24},{1,25},{2,26},{3,27},{4,28},{5,29},{6,30},{7,31},{8,16},{9,... | collective-permute-start | bytes 442376 | tf_op jit(solution)/shard_map/ppermute | solution.py:280
  111.3 4.8 %collective-permute-start.18 = (bf16[144,512]{1,0:T(8,128)(2,1)S(1)}, bf16[144,512]{1,0:T(8,128)(2,1)S(1)}, u32[]{:S(2)}, u32[]{:S(2)}) collective-permute-start(bf16[144,512]{1,0:T(8,128)(2,1)S(1)} %shard_map.88), channel_id=1, source_target_pairs={{0,56},{1,57},{2,58},{3,59},{4,60},{5,61},{6,62},{7,63},{8,48},{9,... | collective-permute-start | bytes 442376 | tf_op jit(solution)/shard_map/ppermute | solution.py:280
  116.2 3.4 %shard_map.90.base_ref = f32[512,512]{1,0:T(8,128)} custom-call(s32[2]{0:T(128)} %pad_add_fusion.at_ref, bf16[512,128]{1,0:T(8,128)(2,1)} %get-tuple-element.99.q_ref, f32[512,128]{1,0:T(8,128)} %copy-done.12, f32[1,512]{1,0:T(1,128)} %bitcast.24, f32[512,512]{1,0:T(8,128)} %shard_map.84.base_ref, bf16[144,512]{1,0:T(8,128)(2,1)} %copy-done.18, ...), custom_call_target="tpu_custom_call" | custom-call | flops 201326592 | bytes 4194304 | tf_op jit(solution)/shard_map/pallas_call | solution.py:45
  119.7 3.6 %shard_map.89.base_ref = f32[512,512]{1,0:T(8,128)} custom-call(s32[2]{0:T(128)} %pad_add_fusion.1.at_ref, bf16[512,128]{1,0:T(8,128)(2,1)} %get-tuple-element.102.q_ref, f32[512,128]{1,0:T(8,128)} %copy-done.10, f32[1,512]{1,0:T(1,128)} %bitcast.25, f32[512,512]{1,0:T(8,128)} %shard_map.86.base_ref, bf16[144,512]{1,0:T(8,128)(2,1)} %copy-done.16, ...), custom_call_target="tpu_custom_call" | custom-call | flops 201326592 | bytes 4194304 | tf_op jit(solution)/shard_map/pallas_call | solution.py:45
  123.3 2.1 %shard_map.92 = (bf16[256,512]{1,0:T(8,128)(2,1)S(1)}, bf16[256,512]{1,0:T(8,128)(2,1)S(1)}) custom-call(s32[3]{0:T(128)S(1)} %add_add_fusion.3.at_ref, bf16[512,128]{1,0:T(8,128)(2,1)S(1)} %copy-done.15, f32[512,128]{1,0:T(8,128)S(1)} %copy-done.13, f32[1,512]{1,0:T(1,128)S(1)} %bitcast.26, f32[512,512]{1,0:T(8,128)S(1)} %copy-done.5, ...), custom_call_target="tpu_custom_call" | custom-call | flops 134217728 | bytes 4194304 | tf_op jit(solution)/shard_map/pallas_call | solution.py:45
  125.5 4.2 %collective-permute-start.21 = (bf16[256,512]{1,0:T(8,128)(2,1)S(1)}, bf16[256,512]{1,0:T(8,128)(2,1)S(1)}, u32[]{:S(2)}, u32[]{:S(2)}) collective-permute-start(bf16[256,512]{1,0:T(8,128)(2,1)S(1)} %get-tuple-element.96), channel_id=1, source_target_pairs={{0,3},{1,2},{2,1},{3,0},{4,7},{5,6},{6,5},{7,4},{8,11},{9,10},{10,... | collective-permute-start | bytes 786440 | tf_op jit(solution)/shard_map/ppermute | solution.py:280
  129.7 2.1 %shard_map.91 = (bf16[256,512]{1,0:T(8,128)(2,1)S(1)}, bf16[256,512]{1,0:T(8,128)(2,1)S(1)}) custom-call(s32[3]{0:T(128)S(1)} %add_add_fusion.at_ref, bf16[512,128]{1,0:T(8,128)(2,1)S(1)} %copy-done.14, f32[512,128]{1,0:T(8,128)S(1)} %copy-done.11, f32[1,512]{1,0:T(1,128)S(1)} %bitcast.27, f32[512,512]{1,0:T(8,128)S(1)} %copy-done.4, ...), custom_call_target="tpu_custom_call" | custom-call | flops 134217728 | bytes 4194304 | tf_op jit(solution)/shard_map/pallas_call | solution.py:45
  131.9 7.3 %collective-permute-done.21.refs_3_ = bf16[256,512]{1,0:T(8,128)(2,1)S(1)} collective-permute-done((bf16[256,512]{1,0:T(8,128)(2,1)S(1)}, bf16[256,512]{1,0:T(8,128)(2,1)S(1)}, u32[]{:S(2)}, u32[]{:S(2)}) %collective-permute-start.21) | collective-permute-done | bytes 262176 | tf_op jit(solution)/shard_map/ppermute | solution.py:280
  (128 shorter events, 34.7 us)
Async XLA Ops:
  0.0 33.0 %collective-permute-start.3 = (bf16[256,4096]{1,0:T(8,128)(2,1)}, bf16[256,4096]{1,0:T(8,128)(2,1)}, u32[]{:S(2)}, u32[]{:S(2)}) collective-permute-start(bf16[256,4096]{1,0:T(8,128)(2,1)} %bitcast.20), channel_id=1, source_target_pairs={{0,1},{1,0},{2,3},{3,2},{4,5},{5,4},{6,7},{7,6},{8,9},{9,8},{10,11... | collective-permute-start | bytes 6291464 | tf_op jit(solution)/shard_map/ppermute | solution.py:280
  5.5 19.9 %collective-permute-start = (bf16[1024,512]{1,0:T(8,128)(2,1)}, bf16[1024,512]{1,0:T(8,128)(2,1)}, u32[]{:S(2)}, u32[]{:S(2)}) collective-permute-start(bf16[1024,512]{1,0:T(8,128)(2,1)} %constant_dynamic-slice_fusion.1.refs_0_), channel_id=1, source_target_pairs={{0,64},{1,193},{2,66},{3,195},{4,68},{5,197},{6,70},{7,199},{8,72}... | collective-permute-start | bytes 3145736 | tf_op jit(solution)/shard_map/ppermute | solution.py:277
  7.9 25.1 %collective-permute-start.2 = (bf16[128,4096]{1,0:T(8,128)(2,1)}, bf16[128,4096]{1,0:T(8,128)(2,1)}, u32[]{:S(2)}, u32[]{:S(2)}) collective-permute-start(bf16[128,4096]{1,0:T(8,128)(2,1)} %get-tuple-element.98), channel_id=1, source_target_pairs={{0,2},{1,3},{2,0},{3,1},{4,6},{5,7},{6,4},{7,5},{8,10},{9,11},{10,... | collective-permute-start | bytes 3145736 | tf_op jit(solution)/shard_map/ppermute | solution.py:280
  10.5 14.9 %collective-permute-start.1 = (bf16[1024,256]{1,0:T(8,128)(2,1)S(1)}, bf16[1024,256]{1,0:T(8,128)(2,1)}, u32[]{:S(2)}, u32[]{:S(2)}) collective-permute-start(bf16[1024,256]{1,0:T(8,128)(2,1)S(1)} %fusion.1.refs_0_), channel_id=1, source_target_pairs={{0,64},{1,193},{2,66},{3,195},{4,68},{5,197},{6,70},{7,199},{8,72}... | collective-permute-start | bytes 1572872 | tf_op jit(solution)/shard_map/ppermute | solution.py:277
  11.1 1.2 collective-permute-start.4
  33.0 27.5 %collective-permute-start.5 = (bf16[1024,512]{1,0:T(8,128)(2,1)}, bf16[1024,512]{1,0:T(8,128)(2,1)}, u32[]{:S(2)}, u32[]{:S(2)}) collective-permute-start(bf16[1024,512]{1,0:T(8,128)(2,1)} %collective-permute-done.refs_1_), channel_id=1, source_target_pairs={{0,64},{1,193},{2,66},{3,195},{4,68},{5,197},{6,70},{7,199},{8,72}... | collective-permute-start | bytes 3145736 | tf_op jit(solution)/shard_map/ppermute | solution.py:277
  33.0 27.5 %collective-permute-start.8 = (bf16[128,4096]{1,0:T(8,128)(2,1)}, bf16[128,4096]{1,0:T(8,128)(2,1)}, u32[]{:S(2)}, u32[]{:S(2)}) collective-permute-start(bf16[128,4096]{1,0:T(8,128)(2,1)} %collective-permute-done.2), channel_id=1, source_target_pairs={{0,1},{1,0},{2,3},{3,2},{4,5},{5,4},{6,7},{7,6},{8,9},{9,8},{10,11... | collective-permute-start | bytes 3145736 | tf_op jit(solution)/shard_map/ppermute | solution.py:280
  34.7 25.8 %collective-permute-start.7 = (bf16[128,4096]{1,0:T(8,128)(2,1)}, bf16[128,4096]{1,0:T(8,128)(2,1)}, u32[]{:S(2)}, u32[]{:S(2)}) collective-permute-start(bf16[128,4096]{1,0:T(8,128)(2,1)} %get-tuple-element.57), channel_id=1, source_target_pairs={{0,2},{1,3},{2,0},{3,1},{4,6},{5,7},{6,4},{7,5},{8,10},{9,11},{10,... | collective-permute-start | bytes 3145736 | tf_op jit(solution)/shard_map/ppermute | solution.py:280
  35.1 25.4 %collective-permute-start.9 = (f32[32,256]{1,0:T(8,128)S(1)}, f32[32,256]{1,0:T(8,128)S(1)}, u32[]{:S(2)}, u32[]{:S(2)}) collective-permute-start(f32[32,256]{1,0:T(8,128)S(1)} %pad_maximum_fusion), channel_id=1, source_target_pairs={{0,2},{1,3},{2,0},{3,1},{4,6},{5,7},{6,4},{7,5},{8,10},{9,11},{10,... | collective-permute-start | bytes 98312 | tf_op jit(solution)/shard_map/ppermute | solution.py:280
  36.6 23.9 %collective-permute-start.6 = (bf16[1024,256]{1,0:T(8,128)(2,1)}, bf16[1024,256]{1,0:T(8,128)(2,1)S(1)}, u32[]{:S(2)}, u32[]{:S(2)}) collective-permute-start(bf16[1024,256]{1,0:T(8,128)(2,1)} %collective-permute-done.1.refs_1_), channel_id=1, source_target_pairs={{0,64},{1,193},{2,66},{3,195},{4,68},{5,197},{6,70},{7,199},{8,72}... | collective-permute-start | bytes 1572872 | tf_op jit(solution)/shard_map/ppermute | solution.py:277
  60.5 18.9 %collective-permute-start.13 = (bf16[128,4096]{1,0:T(8,128)(2,1)}, bf16[128,4096]{1,0:T(8,128)(2,1)S(1)}, u32[]{:S(2)}, u32[]{:S(2)}) collective-permute-start(bf16[128,4096]{1,0:T(8,128)(2,1)} %collective-permute-done.7), channel_id=1, source_target_pairs={{0,1},{1,0},{2,3},{3,2},{4,5},{5,4},{6,7},{7,6},{8,9},{9,8},{10,11... | collective-permute-start | bytes 3145736 | tf_op jit(solution)/shard_map/ppermute | solution.py:280
  61.3 8.3 %collective-permute-start.10 = (bf16[1024,256]{1,0:T(8,128)(2,1)S(1)}, bf16[1024,256]{1,0:T(8,128)(2,1)S(1)}, u32[]{:S(2)}, u32[]{:S(2)}) collective-permute-start(bf16[1024,256]{1,0:T(8,128)(2,1)S(1)} %collective-permute-done.6.refs_2_), channel_id=1, source_target_pairs={{0,64},{1,193},{2,66},{3,195},{4,68},{5,197},{6,70},{7,199},{8,72}... | collective-permute-start | bytes 1572872 | tf_op jit(solution)/shard_map/ppermute | solution.py:277
  64.2 22.9 %collective-permute-start.12 = (bf16[1024,512]{1,0:T(8,128)(2,1)}, bf16[1024,512]{1,0:T(8,128)(2,1)S(1)}, u32[]{:S(2)}, u32[]{:S(2)}) collective-permute-start(bf16[1024,512]{1,0:T(8,128)(2,1)} %collective-permute-done.5.refs_2_.refs_1_), channel_id=1, source_target_pairs={{0,64},{1,193},{2,66},{3,195},{4,68},{5,197},{6,70},{7,199},{8,72}... | collective-permute-start | bytes 3145736 | tf_op jit(solution)/shard_map/ppermute | solution.py:277
  72.7 6.0 %collective-permute-start.11 = (bf16[512,128]{1,0:T(8,128)(2,1)S(1)}, bf16[512,128]{1,0:T(8,128)(2,1)S(1)}, u32[]{:S(2)}, u32[]{:S(2)}) collective-permute-start(bf16[512,128]{1,0:T(8,128)(2,1)S(1)} %get-tuple-element.60), channel_id=1, source_target_pairs={{0,1},{1,0},{2,3},{3,2},{4,5},{5,4},{6,7},{7,6},{8,9},{9,8},{10,11... | collective-permute-start | bytes 393224 | tf_op jit(solution)/shard_map/ppermute | solution.py:280
  82.6 3.8 %collective-permute-start.14 = (bf16[512,128]{1,0:T(8,128)(2,1)S(1)}, bf16[512,128]{1,0:T(8,128)(2,1)S(1)}, u32[]{:S(2)}, u32[]{:S(2)}) collective-permute-start(bf16[512,128]{1,0:T(8,128)(2,1)S(1)} %get-tuple-element.67), channel_id=1, source_target_pairs={{0,1},{1,0},{2,3},{3,2},{4,5},{5,4},{6,7},{7,6},{8,9},{9,8},{10,11... | collective-permute-start | bytes 393224 | tf_op jit(solution)/shard_map/ppermute | solution.py:280
  92.0 12.9 %copy-start.18 = (bf16[144,512]{1,0:T(8,128)(2,1)}, bf16[144,512]{1,0:T(8,128)(2,1)S(1)}, u32[]{:S(2)}) copy-start(bf16[144,512]{1,0:T(8,128)(2,1)S(1)} %get-tuple-element.73.mine_ref.refs_0_) | copy-start | bytes 442372
  93.1 6.2 %collective-permute-start.15 = (bf16[144,512]{1,0:T(8,128)(2,1)S(1)}, bf16[144,512]{1,0:T(8,128)(2,1)S(1)}, u32[]{:S(2)}, u32[]{:S(2)}) collective-permute-start(bf16[144,512]{1,0:T(8,128)(2,1)S(1)} %shard_map.83.mine_ref), channel_id=1, source_target_pairs={{0,6},{1,7},{2,4},{3,5},{4,2},{5,3},{6,0},{7,1},{8,14},{9,15},{10,... | collective-permute-start | bytes 442376 | tf_op jit(solution)/shard_map/ppermute | solution.py:280
  99.4 16.8 %copy-start.6 = (bf16[144,512]{1,0:T(8,128)(2,1)}, bf16[144,512]{1,0:T(8,128)(2,1)S(1)}, u32[]{:S(2)}) copy-start(bf16[144,512]{1,0:T(8,128)(2,1)S(1)} %collective-permute-done.15.got_ref.refs_1_) | copy-start | bytes 442372
  99.5 5.5 %collective-permute-start.16 = (bf16[144,512]{1,0:T(8,128)(2,1)S(1)}, bf16[144,512]{1,0:T(8,128)(2,1)S(1)}, u32[]{:S(2)}, u32[]{:S(2)}) collective-permute-start(bf16[144,512]{1,0:T(8,128)(2,1)S(1)} %shard_map.85.mine_ref), channel_id=1, source_target_pairs={{0,8},{1,9},{2,10},{3,11},{4,12},{5,13},{6,14},{7,15},{8,0},{9,1},... | collective-permute-start | bytes 442376 | tf_op jit(solution)/shard_map/ppermute | solution.py:280
  105.1 6.2 %collective-permute-start.17 = (bf16[144,512]{1,0:T(8,128)(2,1)S(1)}, bf16[144,512]{1,0:T(8,128)(2,1)S(1)}, u32[]{:S(2)}, u32[]{:S(2)}) collective-permute-start(bf16[144,512]{1,0:T(8,128)(2,1)S(1)} %shard_map.87.mine_ref), channel_id=1, source_target_pairs={{0,24},{1,25},{2,26},{3,27},{4,28},{5,29},{6,30},{7,31},{8,16},{9,... | collective-permute-start | bytes 442376 | tf_op jit(solution)/shard_map/ppermute | solution.py:280
  111.3 11.9 %collective-permute-start.18 = (bf16[144,512]{1,0:T(8,128)(2,1)S(1)}, bf16[144,512]{1,0:T(8,128)(2,1)S(1)}, u32[]{:S(2)}, u32[]{:S(2)}) collective-permute-start(bf16[144,512]{1,0:T(8,128)(2,1)S(1)} %shard_map.88), channel_id=1, source_target_pairs={{0,56},{1,57},{2,58},{3,59},{4,60},{5,61},{6,62},{7,63},{8,48},{9,... | collective-permute-start | bytes 442376 | tf_op jit(solution)/shard_map/ppermute | solution.py:280
  125.4 6.5 %collective-permute-start.20 = (bf16[256,512]{1,0:T(8,128)(2,1)S(1)}, bf16[256,512]{1,0:T(8,128)(2,1)S(1)}, u32[]{:S(2)}, u32[]{:S(2)}) collective-permute-start(bf16[256,512]{1,0:T(8,128)(2,1)S(1)} %get-tuple-element.95), channel_id=1, source_target_pairs={{0,2},{1,3},{2,0},{3,1},{4,6},{5,7},{6,4},{7,5},{8,10},{9,11},{10,... | collective-permute-start | bytes 786440 | tf_op jit(solution)/shard_map/ppermute | solution.py:280
  125.5 13.6 %collective-permute-start.21 = (bf16[256,512]{1,0:T(8,128)(2,1)S(1)}, bf16[256,512]{1,0:T(8,128)(2,1)S(1)}, u32[]{:S(2)}, u32[]{:S(2)}) collective-permute-start(bf16[256,512]{1,0:T(8,128)(2,1)S(1)} %get-tuple-element.96), channel_id=1, source_target_pairs={{0,3},{1,2},{2,1},{3,0},{4,7},{5,6},{6,5},{7,4},{8,11},{9,10},{10,... | collective-permute-start | bytes 786440 | tf_op jit(solution)/shard_map/ppermute | solution.py:280
  131.8 7.4 %collective-permute-start.19 = (bf16[256,512]{1,0:T(8,128)(2,1)S(1)}, bf16[256,512]{1,0:T(8,128)(2,1)S(1)}, u32[]{:S(2)}, u32[]{:S(2)}) collective-permute-start(bf16[256,512]{1,0:T(8,128)(2,1)S(1)} %get-tuple-element.93), channel_id=1, source_target_pairs={{0,1},{1,0},{2,3},{3,2},{4,5},{5,4},{6,7},{7,6},{8,9},{9,8},{10,11... | collective-permute-start | bytes 786440 | tf_op jit(solution)/shard_map/ppermute | solution.py:280
  (29 other events, 143.7 us)
